TPU v7x, 32 devices: a whole 2x2x4 slice. The times are simulated.
32 devices in a mesh: batch: 8 (over z, y), shard: 4 (over x, core).
Axes of the slice: x: 2, y: 2, z: 4, core: 2. Of those that a mesh axis runs over, the one named last changes fastest.
Arguments:
- tokens: bfloat16 [2, 32, 1024, 512], P(None, ('batch', 'shard')), may hold values from -6 to 6
- cotangent: bfloat16 [2, 32, 1024, 512], P(None, ('batch', 'shard')), may hold values from -6 to 6
- lengths: int32 [2, 32, 4], P(None, ('batch', 'shard')), may hold values from 1 to 512, 1024 in all within a row
- exit_layers: int32 [2, 32, 4], P(None, ('batch', 'shard')), may hold values from 1 to 8
- teacher: float32 [2, 32, 4, 14], P(None, ('batch', 'shard')), may hold values from -8 to 8
- blocks: bfloat16 [12, 512, 512], P('shard'), may hold values from -0.70710678 to 0.70710678
- left_stats: float32 [12, 512, 512], P('shard'), may hold values from -285212.7 to 6710886.4, as said below
- right_stats: float32 [12, 512, 512], P('shard'), may hold values from -285212.7 to 6710886.4, as said below
- left_root: float32 [12, 512, 512], P('shard'), may hold values from -0.17 to 2, as said below
- right_root: float32 [12, 512, 512], P('shard'), may hold values from -0.17 to 2, as said below
- vectors: float32 [12, 512], P('shard'), may hold values from -1.2 to 1.4
- vec_moment: float32 [12, 512], P('shard'), may hold values from 655.36 to 39321.6
- student: float32 [643, 128], replicated, may hold values from -8 to 8
- stu_moment: float32 [643, 128], replicated, may hold values from 0.512 to 12.8
- classifier: float32 [129, 14], replicated, may hold values from -0.70710677 to 0.70710677
- cls_moment: float32 [129, 14], replicated, may hold values from 0.512 to 12.8
Outputs:
- layer_out: bfloat16 [2, 32, 1024, 512], P(None, ('batch', 'shard'))
- grad_tokens: bfloat16 [2, 32, 1024, 512], P(None, ('batch', 'shard'))
- block_grads: float32 [12, 512, 512], P('shard')
- new_blocks: float32 [12, 512, 512], P('shard')
- new_left: float32 [12, 512, 512], P('shard')
- new_right: float32 [12, 512, 512], P('shard')
- vector_grads: float32 [12, 512], P('shard')
- new_vec_moment: float32 [12, 512], P('shard')
- new_vectors: float32 [12, 512], P('shard')
- student_grads: float32 [643, 128], replicated
- new_stu_moment: float32 [643, 128], replicated
- new_student: float32 [643, 128], replicated
- class_grads: float32 [129, 14], replicated
- new_cls_moment: float32 [129, 14], replicated
- new_classifier: float32 [129, 14], replicated
Inputs may be any that keep to these rules, and one draw needn't show every extreme that they name: In each row the 4 lengths sum to 1024 and the longest is exactly 512. `left_stats`: symmetric. `right_stats`: symmetric. `left_root`: symmetric. `right_root`: symmetric.
All inputs are finite; a program needn't handle non-finite values.
Results may differ from a plain program's by a relative error of at most 0.019.
Values may be sent and summed in bfloat16 or wider, within the bound.
A program may use at most 256 MiB of HBM per device.

v0:
```python
import jax
import jax.numpy as jnp
from jax import lax
from jax.sharding import PartitionSpec as P

D = 512
H = 8
DH = 64
SW = 128
PH = 2
NMAT = 12
SAMP = 4
LAYER = 4


decay_rate = 0.5
block_rate = 0.04
vector_rate = 0.05
head_rate = 0.05


def plain_dot(left_side, right_side):
    return jnp.dot(left_side, right_side, preferred_element_type=jnp.float32)


def inner_dot(left_side, right_side):
    return lax.dot_general(
        left_side, right_side, (((0,), (0,)), ((), ())), preferred_element_type=jnp.float32
    )


def outer_dot(left_side, right_side):
    return lax.dot_general(
        left_side, right_side, (((1,), (1,)), ((), ())), preferred_element_type=jnp.float32
    )


def exact_gelu(values):
    return jax.nn.gelu(values, approximate=False)


def layer_norm(values, gain_vec, shift_vec):
    center = values - jnp.mean(values, axis=-1, keepdims=True)
    spread = jnp.mean(center * center, axis=-1, keepdims=True)
    return center * lax.rsqrt(spread + 1e-06) * gain_vec + shift_vec


def segment_ids(lengths, row_len):
    bounds = jnp.cumsum(lengths, dtype=jnp.int32)
    places = jnp.arange(row_len, dtype=jnp.int32)
    return jnp.sum((places[:, None] >= bounds[None, :]).astype(jnp.int32), axis=1, dtype=jnp.int32)


def head_loss(hidden, segments, alive_flags, target, student, classifier):
    row_count = hidden.shape[0]
    head_width = SW // PH
    pool_weight = student[D : D + SW]
    pool_bias = student[D + SW + 1]
    query_vec = student[D + SW + 2].reshape(PH, head_width)
    split_heads = hidden.reshape(row_count, PH, head_width)
    scores = jnp.sum(split_heads * query_vec, axis=-1) * head_width ** (-0.5)
    member = segments[None, :] == jnp.arange(SAMP, dtype=jnp.int32)[:, None]
    masked = jnp.where(member[:, :, None], scores[None, :, :], -1000000000.0)
    peak_score = jnp.max(masked, axis=1, keepdims=True)
    exponent = jnp.exp(masked - peak_score)
    weights = exponent / jnp.sum(exponent, axis=1, keepdims=True)
    pooled = jnp.einsum(
        "srh,rhc->shc", weights, split_heads, precision=lax.Precision.HIGHEST
    ).reshape(SAMP, SW)
    mixed_head = jnp.tanh(jnp.dot(pooled, pool_weight, precision=lax.Precision.HIGHEST) + pool_bias)
    logits = jnp.dot(mixed_head, classifier[:SW], precision=lax.Precision.HIGHEST) + classifier[SW]
    log_probs = jax.nn.log_softmax(logits, axis=-1)
    return -jnp.sum(alive_flags[:, None] * target * log_probs)


def attend_forward(queries, keys, values, segments):
    row_count, model_width = queries.shape
    span_rows = min(512, row_count)
    block_count = row_count // span_rows
    key_heads = keys.reshape(row_count, H, DH)
    value_heads = values.reshape(row_count, H, DH)

    def one_block(pieces):
        query_part, query_ids = pieces
        scores = jnp.einsum(
            "qhd,khd->hqk",
            query_part.reshape(span_rows, H, DH),
            key_heads,
            preferred_element_type=jnp.float32,
        ) * DH ** (-0.5)
        scores = jnp.where(
            query_ids[None, :, None] == segments[None, None, :], scores, -1000000000.0
        )
        peak_score = jnp.max(scores, axis=-1, keepdims=True)
        exponent = jnp.exp(scores - peak_score)
        total_sum = jnp.sum(exponent, axis=-1, keepdims=True)
        probabilities = (exponent / total_sum).astype(jnp.bfloat16)
        mixed_heads = jnp.einsum(
            "hqk,khd->qhd", probabilities, value_heads, preferred_element_type=jnp.float32
        )
        return (
            mixed_heads.reshape(span_rows, model_width).astype(jnp.bfloat16),
            (peak_score + jnp.log(total_sum))[:, :, 0],
        )

    attended, log_sums = lax.map(
        one_block,
        (
            queries.reshape(block_count, span_rows, model_width),
            segments.reshape(block_count, span_rows),
        ),
    )
    return (attended.reshape(row_count, model_width), log_sums)


def attend_backward(queries, keys, values, segments, log_sums, grad_out):
    row_count, model_width = queries.shape
    span_rows = min(512, row_count)
    block_count = row_count // span_rows
    key_heads = keys.reshape(row_count, H, DH)
    value_heads = values.reshape(row_count, H, DH)

    def one_block(carry, pieces):
        grad_keys, grad_values = carry
        query_part, query_ids, sums_part, grad_part = pieces
        query_heads = query_part.reshape(span_rows, H, DH)
        grad_heads = grad_part.reshape(span_rows, H, DH)
        scores = jnp.einsum(
            "qhd,khd->hqk", query_heads, key_heads, preferred_element_type=jnp.float32
        ) * DH ** (-0.5)
        scores = jnp.where(
            query_ids[None, :, None] == segments[None, None, :], scores, -1000000000.0
        )
        probabilities = jnp.exp(scores - sums_part[:, :, None])
        grad_probs = jnp.einsum(
            "qhd,khd->hqk", grad_heads, value_heads, preferred_element_type=jnp.float32
        )
        inner_sum = jnp.sum(probabilities * grad_probs, axis=-1, keepdims=True)
        grad_scores = (probabilities * (grad_probs - inner_sum)).astype(jnp.bfloat16)
        grad_query = jnp.einsum(
            "hqk,khd->qhd", grad_scores, key_heads, preferred_element_type=jnp.float32
        ) * DH ** (-0.5)
        grad_keys = grad_keys + jnp.einsum(
            "hqk,qhd->khd", grad_scores, query_heads, preferred_element_type=jnp.float32
        ) * DH ** (-0.5)
        grad_values = grad_values + jnp.einsum(
            "hqk,qhd->khd",
            probabilities.astype(jnp.bfloat16),
            grad_heads,
            preferred_element_type=jnp.float32,
        )
        return ((grad_keys, grad_values), grad_query.reshape(span_rows, model_width))

    zero_state = jnp.zeros((row_count, H, DH), jnp.float32)
    (grad_keys, grad_values), grad_queries = lax.scan(
        one_block,
        (zero_state, zero_state),
        (
            queries.reshape(block_count, span_rows, model_width),
            segments.reshape(block_count, span_rows),
            log_sums,
            grad_out.reshape(block_count, span_rows, model_width),
        ),
    )
    return (
        grad_queries.reshape(row_count, model_width),
        grad_keys.reshape(row_count, model_width),
        grad_values.reshape(row_count, model_width),
    )


def send_positions(live_flags, start_place, group_size, slot_count):
    alive_int = (live_flags > 0).astype(jnp.int32)
    rank_index = jnp.cumsum(alive_int, dtype=jnp.int32) - 1
    global_place = start_place + rank_index
    destination = global_place % group_size
    first_place = start_place + (destination - start_place) % group_size
    slot_index = global_place // group_size - first_place // group_size
    return jnp.where(alive_int > 0, destination * slot_count + slot_index, group_size * slot_count)


def receive_positions(start_column, count_column, place_me, group_size, slot_count, span_len):
    first_place = start_column + (place_me - start_column) % group_size
    offset = first_place // group_size
    number = jnp.maximum(
        (start_column + count_column - first_place + group_size - 1) // group_size, 0
    )
    block_ends = offset + number
    places = jnp.arange(span_len, dtype=jnp.int32)
    source = jnp.minimum(
        jnp.sum((block_ends[None, :] <= places[:, None]).astype(jnp.int32), axis=1), group_size - 1
    )
    source_pick = source[:, None] == jnp.arange(group_size, dtype=jnp.int32)[None, :]
    start_of = jnp.sum(jnp.where(source_pick, offset[None, :], 0), axis=1)
    valid_slot = places < block_ends[group_size - 1]
    gather_index = jnp.where(
        valid_slot, source * slot_count + places - start_of, group_size * slot_count
    )
    block_places = jnp.arange(group_size * slot_count, dtype=jnp.int32)
    block_source = block_places // slot_count
    inside = block_places % slot_count
    block_pick = block_source[:, None] == jnp.arange(group_size, dtype=jnp.int32)[None, :]
    block_offset = jnp.sum(jnp.where(block_pick, offset[None, :], 0), axis=1)
    block_number = jnp.sum(jnp.where(block_pick, number[None, :], 0), axis=1)
    back_index = jnp.where(inside < block_number, block_offset + inside, span_len)
    return (gather_index, back_index)


def diagonal_rule(old_values, moment, grads, rate):
    new_moment = decay_rate * moment + (1.0 - decay_rate) * grads * grads
    return (new_moment, old_values - rate * grads / (jnp.sqrt(new_moment) + 1e-08))


def local(
    tokens,
    cotangent,
    lengths,
    exit_layers,
    teacher,
    blocks,
    left_stats,
    right_stats,
    left_root,
    right_root,
    vectors,
    vec_moment,
    student,
    stu_moment,
    classifier,
    cls_moment,
):
    group_size = lax.axis_size("batch")
    place_me = lax.axis_index("batch")
    micro_count, row_count, row_len, model_width = tokens.shape
    span_len = row_count * row_len
    slot_count = span_len // group_size
    segments = jax.vmap(jax.vmap(lambda row_lengths: segment_ids(row_lengths, row_len)))(lengths)
    alive_flags = (exit_layers >= LAYER).astype(jnp.float32)
    member = (segments[..., None] == jnp.arange(SAMP, dtype=jnp.int32)).astype(jnp.float32)
    alive_tok = jnp.sum(member * alive_flags[:, :, None, :], axis=-1)
    counts = jnp.sum(alive_tok, axis=(1, 2)).astype(jnp.int32)
    everyone = lax.all_gather(counts[None, :], "batch", axis=0, tiled=True)
    starts = jnp.cumsum(everyone, axis=0, dtype=jnp.int32) - everyone
    targets = jax.nn.softmax(teacher, axis=-1)
    student_weight = student[:D].astype(jnp.bfloat16)
    student_bias = student[D + SW]
    zero_row = jnp.zeros((1, model_width), jnp.bfloat16)
    grad_blocks = jnp.zeros((NMAT, model_width, model_width), jnp.float32)
    grad_vectors = jnp.zeros((NMAT, model_width), jnp.float32)
    grad_student = jnp.zeros_like(student)
    grad_class = jnp.zeros_like(classifier)
    layer_rows = []
    input_grads = []
    for micro_index in range(micro_count):
        current = (
            lax.all_gather(blocks, "shard", axis=0, tiled=True),
            lax.all_gather(vectors.astype(jnp.bfloat16), "shard", axis=0, tiled=True),
        )
        matrices, vector_low = current
        vector_f32 = vector_low.astype(jnp.float32)
        w_qkv = jnp.concatenate([matrices[0], matrices[1], matrices[2]], axis=1)
        w_out = matrices[3]
        w_up = jnp.concatenate([matrices[4], matrices[5], matrices[6], matrices[7]], axis=1)
        w_down = jnp.concatenate([matrices[8], matrices[9], matrices[10], matrices[11]], axis=0)
        bias_qkv = jnp.concatenate([vector_f32[0], jnp.zeros_like(vector_f32[0]), vector_f32[1]])
        flat_in = tokens[micro_index].reshape(span_len, model_width)
        seg_now = segments[micro_index]
        projected = (plain_dot(flat_in, w_qkv) + bias_qkv).astype(jnp.bfloat16)
        queries = projected[:, :model_width].reshape(row_count, row_len, model_width)
        keys = projected[:, model_width : 2 * model_width].reshape(row_count, row_len, model_width)
        values = projected[:, 2 * model_width :].reshape(row_count, row_len, model_width)
        attended, log_sums = jax.vmap(attend_forward)(queries, keys, values, seg_now)
        attended = attended.reshape(span_len, model_width)
        first_in = flat_in.astype(jnp.float32) + (plain_dot(attended, w_out) + vector_f32[2])
        first_norm, first_pull = jax.vjp(layer_norm, first_in, vector_f32[3], vector_f32[4])
        first_low = first_norm.astype(jnp.bfloat16)
        hidden = plain_dot(first_low, w_up) + vector_f32[5:9].reshape(-1)
        activated, gelu_pull = jax.vjp(exact_gelu, hidden)
        activated_low = activated.astype(jnp.bfloat16)
        second_in = first_norm + (plain_dot(activated_low, w_down) + vector_f32[9])
        normed, second_pull = jax.vjp(layer_norm, second_in, vector_f32[10], vector_f32[11])
        normed_low = normed.astype(jnp.bfloat16)
        head_in = plain_dot(normed_low, student_weight) + student_bias
        alive_now = alive_flags[micro_index]
        target_now = targets[micro_index]

        def head_total(head_values, student_now, classifier_now):
            losses = jax.vmap(head_loss, in_axes=(0, 0, 0, 0, None, None))(
                head_values.reshape(row_count, row_len, SW),
                seg_now,
                alive_now,
                target_now,
                student_now,
                classifier_now,
            )
            return jnp.sum(losses)

        head_value, head_pull = jax.vjp(head_total, head_in, student, classifier)
        grad_head, grad_student_part, grad_class_part = head_pull(jnp.ones((), jnp.float32))
        grad_head_low = grad_head.astype(jnp.bfloat16)
        grad_student = grad_student + grad_student_part
        grad_student = grad_student.at[:D].add(inner_dot(normed_low, grad_head_low))
        grad_student = grad_student.at[D + SW].add(
            jnp.sum(grad_head_low.astype(jnp.float32), axis=0)
        )
        grad_class = grad_class + grad_class_part
        grad_normed = outer_dot(grad_head_low, student_weight)
        send_index = send_positions(
            alive_tok[micro_index].reshape(span_len),
            starts[place_me, micro_index],
            group_size,
            slot_count,
        )
        gather_index, back_index = receive_positions(
            starts[:, micro_index],
            everyone[:, micro_index],
            place_me,
            group_size,
            slot_count,
            span_len,
        )
        outgoing = (
            jnp.zeros((group_size * slot_count + 1, model_width), jnp.bfloat16)
            .at[send_index]
            .set(normed_low)[: group_size * slot_count]
        )
        arrived = lax.all_to_all(
            outgoing.reshape(group_size, slot_count, model_width),
            "batch",
            split_axis=0,
            concat_axis=0,
            tiled=True,
        )
        arrived_rows = jnp.concatenate(
            [arrived.reshape(group_size * slot_count, model_width), zero_row]
        )
        layer_rows.append(arrived_rows[gather_index].reshape(row_count, row_len, model_width))
        cot_rows = jnp.concatenate(
            [cotangent[micro_index].reshape(span_len, model_width), zero_row]
        )
        grad_outgoing = cot_rows[back_index]
        returned = lax.all_to_all(
            grad_outgoing.reshape(group_size, slot_count, model_width),
            "batch",
            split_axis=0,
            concat_axis=0,
            tiled=True,
        )
        returned_rows = jnp.concatenate(
            [returned.reshape(group_size * slot_count, model_width), zero_row]
        )
        grad_normed = grad_normed + returned_rows[send_index].astype(jnp.float32)
        grad_second, grad_gain_two, grad_shift_two = second_pull(grad_normed)
        grad_feed_low = grad_second.astype(jnp.bfloat16)
        grad_down_bias = jnp.sum(grad_feed_low.astype(jnp.float32), axis=0)
        grad_down = inner_dot(activated_low, grad_feed_low)
        grad_activated = outer_dot(grad_feed_low, w_down)
        grad_hidden_low = gelu_pull(grad_activated)[0].astype(jnp.bfloat16)
        grad_up_bias = jnp.sum(grad_hidden_low.astype(jnp.float32), axis=0)
        grad_up = inner_dot(first_low, grad_hidden_low)
        grad_first = grad_second + outer_dot(grad_hidden_low, w_up)
        grad_first_in, grad_gain_one, grad_shift_one = first_pull(grad_first)
        grad_branch_low = grad_first_in.astype(jnp.bfloat16)
        grad_out_bias = jnp.sum(grad_branch_low.astype(jnp.float32), axis=0)
        grad_out_weight = inner_dot(attended, grad_branch_low)
        grad_attended = outer_dot(grad_branch_low, w_out).astype(jnp.bfloat16)
        grad_query, grad_key, grad_value = jax.vmap(attend_backward)(
            queries,
            keys,
            values,
            seg_now,
            log_sums,
            grad_attended.reshape(row_count, row_len, model_width),
        )
        grad_proj_low = jnp.concatenate(
            [
                grad_query.reshape(span_len, model_width),
                grad_key.reshape(span_len, model_width),
                grad_value.reshape(span_len, model_width),
            ],
            axis=1,
        ).astype(jnp.bfloat16)
        grad_proj_sum = jnp.sum(grad_proj_low.astype(jnp.float32), axis=0)
        grad_qkv = inner_dot(flat_in, grad_proj_low)
        grad_input = grad_first_in + outer_dot(grad_proj_low, w_qkv)
        input_grads.append(grad_input.astype(jnp.bfloat16).reshape(row_count, row_len, model_width))
        grad_blocks = grad_blocks + jnp.stack(
            [
                grad_qkv[:, :model_width],
                grad_qkv[:, model_width : 2 * model_width],
                grad_qkv[:, 2 * model_width :],
                grad_out_weight,
            ]
            + [
                grad_up[:, part_index * model_width : (part_index + 1) * model_width]
                for part_index in range(4)
            ]
            + [
                grad_down[part_index * model_width : (part_index + 1) * model_width]
                for part_index in range(4)
            ]
        )
        grad_vectors = grad_vectors + jnp.stack(
            [
                grad_proj_sum[:model_width],
                grad_proj_sum[2 * model_width :],
                grad_out_bias,
                grad_gain_one,
                grad_shift_one,
            ]
            + [
                grad_up_bias[part_index * model_width : (part_index + 1) * model_width]
                for part_index in range(4)
            ]
            + [grad_down_bias, grad_gain_two, grad_shift_two]
        )
    whole_blocks, whole_vectors = lax.psum((grad_blocks, grad_vectors), "batch")
    owned_blocks, owned_vectors = (
        lax.psum_scatter(
            whole_blocks.astype(jnp.bfloat16), "shard", scatter_dimension=0, tiled=True
        ).astype(jnp.float32),
        lax.psum_scatter(
            whole_vectors.astype(jnp.bfloat16), "shard", scatter_dimension=0, tiled=True
        ).astype(jnp.float32),
    )
    head_student, head_class = lax.psum((grad_student, grad_class), ("batch", "shard"))
    gram_left = jnp.einsum(
        "bij,bkj->bik", owned_blocks, owned_blocks, precision=lax.Precision.HIGHEST
    )
    gram_right = jnp.einsum(
        "bji,bjk->bik", owned_blocks, owned_blocks, precision=lax.Precision.HIGHEST
    )
    new_left = decay_rate * left_stats + (1.0 - decay_rate) * gram_left
    new_right = decay_rate * right_stats + (1.0 - decay_rate) * gram_right
    steered = jnp.einsum("bij,bjk->bik", left_root, owned_blocks, precision=lax.Precision.HIGHEST)
    steered = jnp.einsum("bij,bjk->bik", steered, right_root, precision=lax.Precision.HIGHEST)
    size_norm = jnp.sqrt(jnp.mean(steered * steered, axis=(1, 2), keepdims=True) + 1e-06)
    new_blocks = blocks.astype(jnp.float32) - block_rate * steered / size_norm
    new_vec_moment, new_vectors = diagonal_rule(vectors, vec_moment, owned_vectors, vector_rate)
    new_stu_moment, new_student = diagonal_rule(student, stu_moment, head_student, head_rate)
    new_cls_moment, new_classifier = diagonal_rule(classifier, cls_moment, head_class, head_rate)
    return (
        jnp.stack(layer_rows),
        jnp.stack(input_grads),
        owned_blocks,
        new_blocks,
        new_left,
        new_right,
        owned_vectors,
        new_vec_moment,
        new_vectors,
        head_student,
        new_stu_moment,
        new_student,
        head_class,
        new_cls_moment,
        new_classifier,
    )


def solution(mesh):
    return jax.shard_map(
        local,
        mesh=mesh,
        in_specs=(
            P(None, ("batch", "shard"), None, None),
            P(None, ("batch", "shard"), None, None),
            P(None, ("batch", "shard"), None),
            P(None, ("batch", "shard"), None),
            P(None, ("batch", "shard"), None, None),
            P("shard", None, None),
            P("shard", None, None),
            P("shard", None, None),
            P("shard", None, None),
            P("shard", None, None),
            P("shard", None),
            P("shard", None),
            P(),
            P(),
            P(),
            P(),
        ),
        out_specs=(
            P(None, ("batch", "shard"), None, None),
            P(None, ("batch", "shard"), None, None),
            P("shard", None, None),
            P("shard", None, None),
            P("shard", None, None),
            P("shard", None, None),
            P("shard", None),
            P("shard", None),
            P("shard", None),
            P(),
            P(),
            P(),
            P(),
            P(),
            P(),
        ),
        check_vma=False,
    )
```

profile of v0, /device:TPU:0, one launch (start us, length us, event | category | flops | bytes accessed | tf_op | source)
XLA Modules:
  0.0 1378.9 jit_solution(5376848085700333540)
XLA Ops:
  11.9 13.1 all-reduce.16
  31.8 6.5 gather_fusion.2
  51.0 6.5 gather_fusion.4
  86.5 6.5 gather_fusion.3
  126.8 40.7 %while.59 = (s32[]{:T(128)}, bf16[2,1,512,512]{3,2,0,1:T(8,128)(2,1)}, f32[2,1,8,512]{3,2,1,0:T(8,128)S(1)}, s32[2,1,512]{2,1,0:T(1,128)S(1)}, s32[1,1,1024]{2,1...) while((s32[]{:T(128)}, ...), condition=%wide.region_23.24_spmd, body=%wide.region_20.23_spmd.sunk | while | flops 1124855808 | bytes 63056016 | solution.py:106
  180.9 40.4 %while.58 = (s32[]{:T(128)}, bf16[2,1,512,512]{3,2,0,1:T(8,128)(2,1)}, f32[2,1,8,512]{3,2,1,0:T(8,128)S(1)}, s32[2,1,512]{2,1,0:T(1,128)S(1)}, s32[1,1,1024]{2,1...) while((s32[]{:T(128)}, ...), condition=%wide.region_10.11_spmd, body=%wide.region_7.10_spmd.sunk | while | flops 1124855808 | bytes 63056016 | solution.py:106
  227.6 42.8 %multiply_convert_fusion.3 = (bf16[1024,2048]{1,0:T(8,128)(2,1)S(1)}, f32[1024,2048]{1,0:T(8,128)}, bf16[1024,2048]{1,0:T(8,128)(2,1)S(1)}, f32[1024,2048]{1,0:T(8,128)}, f32[1024,2048]{1,0:T(8,128)}) fusion(f32[2048]{0:T(1024)S(1)} %bitcast.759, f32[1024,2048]{1,0:T(8,128)S(1)} %fusion.154, bf16[512,512]{1,0:T(8,128)(2,1)S(1)} %copy-done.60, ...), kind=kOutput, calls=%fused_computation.99 | convolution fusion | flops 2432696320 | bytes 45096960 | tf_op jit(solution)/shard_map/dot_general | solution.py:23
  328.8 12.6 convert_reduce_fusion
  353.9 12.4 convert_reduce_fusion.1
  385.5 129.5 %while.61 = (s32[]{:T(128)}, f32[1,1024,8,64]{1,3,2,0:T(8,128)}, f32[1,1024,8,64]{1,3,2,0:T(8,128)}, bf16[2,1,512,512]{3,2,0,1:T(8,128)(2,1)}, bf16[2,1,512,512]...) while((s32[]{:T(128)}, f32[1,1024,8,64]{1,3,2,0:T(8,128)}, ...), condition=%wide.region_70.71_spmd.clone, body=%wide.region_68.70_spmd.clone.sunk | while | flops 2725769216 | bytes 272197984 | solution.py:155
  391.9 9.6 fusion.342
  401.5 12.6 multiply_reduce_fusion.20
  414.1 15.0 %multiply_convert_fusion.7 = bf16[8,512,1024]{2,1,0:T(8,128)(2,1)} fusion(f32[8,512,1024]{2,1,0:T(8,128)} %get-tuple-element.1131, f32[8,512,1024]{2,1,0:T(8,128)} %fusion.342, f32[8,512]{1,0:T(8,128)S(1)} %get-tuple-element.1132), kind=kLoop, calls=%fused_computation.60.clone.1 | loop fusion | flops 12582912 | bytes 41959424 | tf_op jit(solution)/shard_map/vmap()/while/body/eval_jaxpr/convert_element_type | solution.py:139
  435.4 7.0 convolution_multiply_fusion.7
  455.6 9.6 fusion.342
  465.2 12.6 multiply_reduce_fusion.20
  477.8 15.0 %multiply_convert_fusion.7 = bf16[8,512,1024]{2,1,0:T(8,128)(2,1)} fusion(f32[8,512,1024]{2,1,0:T(8,128)} %get-tuple-element.1131, f32[8,512,1024]{2,1,0:T(8,128)} %fusion.342, f32[8,512]{1,0:T(8,128)S(1)} %get-tuple-element.1132), kind=kLoop, calls=%fused_computation.60.clone.1 | loop fusion | flops 12582912 | bytes 41959424 | tf_op jit(solution)/shard_map/vmap()/while/body/eval_jaxpr/convert_element_type | solution.py:139
  500.9 7.0 convolution_multiply_fusion.7
  539.6 129.5 %while.60 = (s32[]{:T(128)}, f32[1,1024,8,64]{1,3,2,0:T(8,128)}, f32[1,1024,8,64]{1,3,2,0:T(8,128)}, bf16[2,1,512,512]{3,2,0,1:T(8,128)(2,1)}, bf16[2,1,512,512]...) while((s32[]{:T(128)}, f32[1,1024,8,64]{1,3,2,0:T(8,128)}, ...), condition=%wide.region_51.52_spmd.clone, body=%wide.region_49.51_spmd.clone.sunk | while | flops 2725769216 | bytes 272197984 | solution.py:155
  545.9 9.6 fusion.332
  555.4 12.6 multiply_reduce_fusion.19
  568.0 15.0 %multiply_convert_fusion.6 = bf16[8,512,1024]{2,1,0:T(8,128)(2,1)} fusion(f32[8,512,1024]{2,1,0:T(8,128)} %get-tuple-element.1118, f32[8,512,1024]{2,1,0:T(8,128)} %fusion.332, f32[8,512]{1,0:T(8,128)S(1)} %get-tuple-element.1119), kind=kLoop, calls=%fused_computation.42.clone.1 | loop fusion | flops 12582912 | bytes 41959424 | tf_op jit(solution)/shard_map/vmap()/while/body/eval_jaxpr/convert_element_type | solution.py:139
  589.4 7.0 convolution_multiply_fusion.6
  609.7 9.6 fusion.332
  619.3 12.6 multiply_reduce_fusion.19
  631.9 15.0 %multiply_convert_fusion.6 = bf16[8,512,1024]{2,1,0:T(8,128)(2,1)} fusion(f32[8,512,1024]{2,1,0:T(8,128)} %get-tuple-element.1118, f32[8,512,1024]{2,1,0:T(8,128)} %fusion.332, f32[8,512]{1,0:T(8,128)S(1)} %get-tuple-element.1119), kind=kLoop, calls=%fused_computation.42.clone.1 | loop fusion | flops 12582912 | bytes 41959424 | tf_op jit(solution)/shard_map/vmap()/while/body/eval_jaxpr/convert_element_type | solution.py:139
  655.0 7.0 convolution_multiply_fusion.6
  724.0 488.6 %all-reduce.23 = (bf16[12,512,512]{1,2,0:T(8,128)(2,1)}, bf16[12,512]{1,0:T(8,128)(2,1)}) all-reduce(f32[12,512,512]{1,2,0:T(8,128)} %add.954, f32[12,512]{1,0:T(8,128)S(1)} %add.958), channel_id=1, replica_groups=mesh['batch'=8,'shard'=4] {'batch'}, use_global_device_ids=true, to_apply=%region_71.72 | all-reduce | flops 3151872 | bytes 18911232 | tf_op jit(solution)/shard_map/psum | solution.py:417
  1215.0 6.6 scatter_custom_fusion
  1235.2 6.6 scatter_custom_fusion.1
  1270.3 40.8 %psum.31 = f32[129,14]{0,1:T(8,128)S(1)} all-reduce(f32[129,14]{0,1:T(8,128)S(1)} %add_add_fusion.11), channel_id=1, replica_groups=mesh['batch'=8,'shard'=4] {'batch','shard'}, use_global_device_ids=true, to_apply=%region_101.102 | all-reduce | flops 1806 | bytes 14448 | tf_op jit(solution)/shard_map/psum | solution.py:426
  1311.1 11.0 all-reduce.17
  (753 shorter events, 529.7 us)
Async XLA Ops:
  7.2 1344.6 %copy-start = (f32[3,512,512]{2,1,0:T(8,128)S(1)}, f32[3,512,512]{2,1,0:T(8,128)}, u32[]{:S(2)}) copy-start(f32[3,512,512]{2,1,0:T(8,128)} %param.41) | copy-start | bytes 9437188
  7.2 100.8 %all-gather.4.cloned.1.call-start = ((), (), s32[]{:S(2)}) async-start(), calls=%async_computation.5 | async-start | bytes 7864320 | tf_op jit(solution)/shard_map/all_gather | solution.py:256
  38.3 28.0 %all-to-all-start.2 = ((bf16[8,128,512]{2,1,0:T(8,128)(2,1)}), bf16[8,128,512]{2,1,0:T(8,128)(2,1)}, u32[]{:S(2)}, u32[]{:S(2)}) async-start(bf16[8,128,512]{2,1,0:T(8,128)(2,1)} %bitcast.680), calls=%async_computation.2 | async-start | bytes 2097152 | tf_op jit(solution)/shard_map/all_to_all | solution.py:342
  66.3 30.7 %all-to-all-start.3 = ((bf16[8,128,512]{2,1,0:T(8,128)(2,1)}), bf16[8,128,512]{2,1,0:T(8,128)(2,1)}, u32[]{:S(2)}, u32[]{:S(2)}) async-start(bf16[8,128,512]{2,1,0:T(8,128)(2,1)} %bitcast.679), calls=%async_computation.3 | async-start | bytes 2097152 | tf_op jit(solution)/shard_map/all_to_all | solution.py:342
  70.7 1253.4 %all-reduce.22.cloned.1.call-start = ((), (), s32[]{:S(2)}) async-start(), calls=%async_computation.7 | async-start | bytes 663552 | tf_op jit(solution)/shard_map/psum | solution.py:426
  126.8 40.7 %copy-start.163 = (f32[1,512]{1,0:T(1,128)S(1)}, f32[1,512]{1,0:T(1,128)}, u32[]{:S(2)}) copy-start(f32[1,512]{1,0:T(1,128)} %get-tuple-element.802) | copy-start | bytes 6148
  180.9 40.5 %copy-start.164 = (f32[1,512]{1,0:T(1,128)S(1)}, f32[1,512]{1,0:T(1,128)}, u32[]{:S(2)}) copy-start(f32[1,512]{1,0:T(1,128)} %get-tuple-element.802) | copy-start | bytes 6148
  224.1 46.4 %copy-start.22 = (f32[1024,512]{0,1:T(8,128)}, f32[1024,512]{0,1:T(8,128)S(1)}, u32[]{:S(2)}) copy-start(f32[1024,512]{0,1:T(8,128)S(1)} %get-tuple-element.850) | copy-start | bytes 6291460
  224.1 46.4 %copy-start.98 = (f32[1024]{0:T(1024)}, f32[1024]{0:T(1024)S(1)}, u32[]{:S(2)}) copy-start(f32[1024]{0:T(1024)S(1)} %broadcast_multiply_fusion.9) | copy-start | bytes 12292
  224.4 46.1 %copy-start.108 = (f32[1024]{0:T(1024)}, f32[1024]{0:T(1024)S(1)}, u32[]{:S(2)}) copy-start(f32[1024]{0:T(1024)S(1)} %fusion.118) | copy-start | bytes 12292
  227.6 42.8 %copy-start.175 = (f32[1024,2048]{1,0:T(8,128)}, f32[1024,2048]{1,0:T(8,128)S(1)}, u32[]{:S(2)}) copy-start(f32[1024,2048]{1,0:T(8,128)S(1)} %fusion.154) | copy-start | bytes 25165828
  227.6 42.9 %copy-start.68 = (bf16[512,512]{1,0:T(8,128)(2,1)S(1)}, bf16[512,512]{1,0:T(8,128)(2,1)}, u32[]{:S(2)}) copy-start(bf16[512,512]{1,0:T(8,128)(2,1)} %get-tuple-element.773) | copy-start | bytes 1572868
  227.6 42.9 %copy-start.70 = (bf16[512,512]{1,0:T(8,128)(2,1)S(1)}, bf16[512,512]{1,0:T(8,128)(2,1)}, u32[]{:S(2)}) copy-start(bf16[512,512]{1,0:T(8,128)(2,1)} %get-tuple-element.774) | copy-start | bytes 1572868
  227.6 42.9 %copy-start.72 = (bf16[512,512]{1,0:T(8,128)(2,1)S(1)}, bf16[512,512]{1,0:T(8,128)(2,1)}, u32[]{:S(2)}) copy-start(bf16[512,512]{1,0:T(8,128)(2,1)} %get-tuple-element.775) | copy-start | bytes 1572868
  227.6 42.9 %copy-start.74 = (bf16[512,512]{1,0:T(8,128)(2,1)S(1)}, bf16[512,512]{1,0:T(8,128)(2,1)}, u32[]{:S(2)}) copy-start(bf16[512,512]{1,0:T(8,128)(2,1)} %get-tuple-element.776) | copy-start | bytes 1572868
  227.6 42.9 %copy-start.162 = (f32[1,512]{1,0:T(1,128)S(1)}, f32[1,512]{1,0:T(1,128)}, u32[]{:S(2)}) copy-start(f32[1,512]{1,0:T(1,128)} %get-tuple-element.799) | copy-start | bytes 6148
  291.1 28.5 %copy-start.19 = (f32[1024,512]{0,1:T(8,128)S(1)}, f32[1024,512]{0,1:T(8,128)}, u32[]{:S(2)}) copy-start(f32[1024,512]{0,1:T(8,128)} %copy-done.18) | copy-start | bytes 6291460
  291.1 28.5 %copy-start.21 = (f32[1024,512]{0,1:T(8,128)S(1)}, f32[1024,512]{0,1:T(8,128)}, u32[]{:S(2)}) copy-start(f32[1024,512]{0,1:T(8,128)} %copy-done.20) | copy-start | bytes 6291460
  291.1 28.8 %copy-start.40 = (bf16[1024,512]{0,1:T(8,128)(2,1)S(1)}, bf16[1024,512]{0,1:T(8,128)(2,1)}, u32[]{:S(2)}) copy-start(bf16[1024,512]{0,1:T(8,128)(2,1)} %copy.244) | copy-start | bytes 3145732
  291.1 28.8 %copy-start.95 = (f32[1024]{0:T(1024)S(1)}, f32[1024]{0:T(1024)}, u32[]{:S(2)}) copy-start(f32[1024]{0:T(1024)} %copy-done.94) | copy-start | bytes 12292
  291.1 28.8 %copy-start.97 = (f32[1024]{0:T(1024)S(1)}, f32[1024]{0:T(1024)}, u32[]{:S(2)}) copy-start(f32[1024]{0:T(1024)} %copy-done.96) | copy-start | bytes 12292
  291.1 28.8 %copy-start.102 = (f32[1024]{0:T(1024)S(1)}, f32[1024]{0:T(1024)}, u32[]{:S(2)}) copy-start(f32[1024]{0:T(1024)} %copy-done.101) | copy-start | bytes 12292
  291.1 28.8 %copy-start.104 = (f32[1024]{0:T(1024)S(1)}, f32[1024]{0:T(1024)}, u32[]{:S(2)}) copy-start(f32[1024]{0:T(1024)} %copy-done.103) | copy-start | bytes 12292
  291.1 28.8 %copy-start.123 = (f32[1,512]{1,0:T(1,128)S(1)}, f32[1,512]{1,0:T(1,128)}, u32[]{:S(2)}) copy-start(f32[1,512]{1,0:T(1,128)} %get-tuple-element.797) | copy-start | bytes 6148
  698.6 648.2 %reduce-scatter.2.cloned.1.call-start = ((), (), s32[]{:S(2)}) async-start(), calls=%async_computation.6 | async-start | bytes 7864320 | tf_op jit(solution)/shard_map/reduce_scatter | solution.py:419
  1224.1 30.9 %all-to-all-start = ((bf16[8,128,512]{2,1,0:T(8,128)(2,1)}), bf16[8,128,512]{2,1,0:T(8,128)(2,1)}, u32[]{:S(2)}, u32[]{:S(2)}) async-start(bf16[8,128,512]{2,1,0:T(8,128)(2,1)} %bitcast.692), calls=%async_computation | async-start | bytes 2097152 | tf_op jit(solution)/shard_map/all_to_all | solution.py:327
  1255.0 79.9 %all-to-all-start.1 = ((bf16[8,128,512]{2,1,0:T(8,128)(2,1)}), bf16[8,128,512]{2,1,0:T(8,128)(2,1)}, u32[]{:S(2)}, u32[]{:S(2)}) async-start(bf16[8,128,512]{2,1,0:T(8,128)(2,1)} %bitcast.691), calls=%async_computation.1 | async-start | bytes 2097152 | tf_op jit(solution)/shard_map/all_to_all | solution.py:327
  1264.4 57.7 %copy-start.121 = (f32[3,512]{1,0:T(4,128)S(1)}, f32[3,512]{1,0:T(4,128)}, u32[]{:S(2)}) copy-start(f32[3,512]{1,0:T(4,128)} %param.42) | copy-start | bytes 18436
  1264.4 57.7 %copy-start.153 = (f32[3,512]{1,0:T(4,128)S(1)}, f32[3,512]{1,0:T(4,128)}, u32[]{:S(2)}) copy-start(f32[3,512]{1,0:T(4,128)} %param.43) | copy-start | bytes 18436
  1264.4 58.4 %copy-start.87 = (f32[129,14]{0,1:T(8,128)S(1)}, f32[129,14]{0,1:T(8,128)}, u32[]{:S(2)}) copy-start(f32[129,14]{0,1:T(8,128)} %param.46) | copy-start | bytes 21676
  1264.4 59.7 %copy-start.34 = (f32[643,128]{1,0:T(8,128)S(1)}, f32[643,128]{1,0:T(8,128)}, u32[]{:S(2)}) copy-start(f32[643,128]{1,0:T(8,128)} %param.44) | copy-start | bytes 987652
  1311.1 23.9 %copy-start.100 = (f32[129,14]{0,1:T(8,128)}, f32[129,14]{0,1:T(8,128)S(1)}, u32[]{:S(2)}) copy-start(f32[129,14]{0,1:T(8,128)S(1)} %psum.31) | copy-start | bytes 21676
  (171 other events, 1170.6 us)
Sparse Core Ops, SparseCore 0:
  9.6 49.1 all-gather.3
  698.7 160.0 all-reduce.21
  1212.8 57.0 reduce-scatter.1
where the time goes:
time: 1390 us; the launch traced here: 1380 us
  blocking collectives  559 us (40%)
  matrix products  370 us (27%)
  local copies, waits for them, and re-layouts  249 us (18%)
  other arithmetic  156 us (11%)
  starting transfers between devices  17.7 us (1%)
  between operations  17.7 us (1%)
    psum x1, blocking collectives, local(): whole_blocks, whole_vectors = lax.psum((grad_blocks, grad_vectors), 'batch')  489 us
    dot_general x10, matrix products, plain_dot(): return jnp.dot(left_side, right_side, preferred_element_type=jnp.float32)  63 us
    convert_element_type x4, other arithmetic, one_block(): (probabilities * (grad_probs - inner_sum)).astype(jnp.bfloat16)  60 us
    dot_general x10, matrix products, outer_dot(): lax.dot_general(left_side, right_side, (((1,), (1,)), ((), ())), preferre...  52.3 us
    dot_general x4, matrix products, one_block(): jnp.einsum('qhd,khd->hqk', query_heads, key_heads, preferred_element_type...  50.2 us
    psum x1, blocking collectives, local(): lax.psum((grad_student, grad_class), ('batch', 'shard'))  40.8 us
    dot_general x4, matrix products, one_block(): jnp.einsum('qhd,khd->hqk', grad_heads, value_heads, preferred_element_typ...  38.3 us
    unnamed x358, local copies, waits for them, and re-layouts  37.4 us
  transfers between devices with their start and end apart: 7, of which 3 were waited for; matrix products, arithmetic and copies ran while one was open for 11% of the time, Pallas kernels for 0%

commit v1 on v0

v1 whole, which is shorter than its diff:
```python
import functools

import jax
import jax.numpy as jnp
from jax import lax
from jax.experimental import pallas as pl
from jax.experimental.pallas import tpu as pltpu
from jax.sharding import PartitionSpec as P

D = 512
H = 8
DH = 64
FF = 2048
SW = 128
NMAT = 12
SAMP = 4
LAYER = 4
CLS = 14

decay_rate = 0.5
block_rate = 0.04
vector_rate = 0.05
head_rate = 0.05

QT = 256
KG = 128
PAIRS = H // 2
LANES = 128
BIG = float(2**30)
EPS = 1e-6
VMEM = 60 * 1024 * 1024

F32 = jnp.float32
BF16 = jnp.bfloat16


def nn(a, b):
    return jnp.dot(a, b, preferred_element_type=F32)


def nt(a, b):
    return lax.dot_general(a, b, (((1,), (1,)), ((), ())), preferred_element_type=F32)


def tn(a, b):
    return lax.dot_general(a, b, (((0,), (0,)), ((), ())), preferred_element_type=F32)


def exact(a, b, dims=(((1,), (0,)), ((), ()))):
    return lax.dot_general(
        a, b, dims, preferred_element_type=F32, precision=lax.Precision.HIGHEST
    )


def row_sum(v):
    return jnp.sum(v, axis=0, keepdims=True)


def split_low(v):
    high = v.astype(BF16).astype(F32)
    rest = v - high
    mid = rest.astype(BF16).astype(F32)
    return high, mid, rest - mid


def ends_of(info, row):
    return [info[row, j] for j in range(SAMP)]


def live_of(info, row):
    return [info[row, SAMP + j] for j in range(SAMP)]


def sample_column(ends, first, count):
    place = first + lax.broadcasted_iota(jnp.int32, (count, 1), 0)
    total = jnp.zeros((count, 1), jnp.int32)
    for j in range(SAMP - 1):
        total = total + (place >= ends[j]).astype(jnp.int32)
    return total


def reach(ends, live, first, count, row_len):
    low, high = jnp.int32(row_len), jnp.int32(0)
    start = jnp.int32(0)
    for j in range(SAMP):
        end = ends[j]
        meets = (start < first + count) & (end > first) & (end > start) & (live[j] > 0)
        low = jnp.where(meets, jnp.minimum(low, start), low)
        high = jnp.where(meets, jnp.maximum(high, end), high)
        start = end
    begin = low // KG
    number = jnp.maximum((high + KG - 1) // KG - begin, 0)
    return begin, number


def lane_index(rows):
    return lax.broadcasted_iota(jnp.int32, (rows, LANES), 1)


def key_spare(sample, rows):
    lane = lane_index(rows) % DH
    return jnp.where(
        lane < SAMP, (lane == sample).astype(F32), (lane < SAMP + 3).astype(F32)
    )


def query_spare(sample, rows):
    lane = lane_index(rows) % DH
    return jnp.where((lane < SAMP) & (lane != sample), -BIG, 0.0)


def halves(pair, spare, first):
    return jnp.where(first, pair, spare), jnp.where(first, spare, pair)


def attend_kernel(
    info, x_ref, w_ref, vec_ref, a1_ref, q_ref, k_ref, v_ref, o_ref, kx, vx
):
    row = pl.program_id(0)
    row_len = x_ref.shape[1]
    ends, live = ends_of(info, row), live_of(info, row)
    first = lane_index(QT) < DH

    @pl.loop(0, row_len // QT)
    def _(t):
        rows = pl.ds(pl.multiple_of(t * QT, QT), QT)
        x = x_ref[0, rows, :]
        sample = sample_column(ends, t * QT, QT)
        k_extra, q_extra = key_spare(sample, QT), query_spare(sample, QT)
        q = (nn(x, w_ref[0]) + vec_ref[0:1, :]).astype(BF16).astype(F32) * DH**-0.5
        k = nn(x, w_ref[1]).astype(BF16)
        v = (nn(x, w_ref[2]) + vec_ref[1:2, :]).astype(BF16)
        k_ref[0, rows, :] = k
        v_ref[0, rows, :] = v
        for p in range(PAIRS):
            pair = slice(p * LANES, (p + 1) * LANES)
            for ref, values, spare in (
                (q_ref.at[0], q, q_extra),
                (kx, k.astype(F32), k_extra),
                (vx, v.astype(F32), jnp.ones((QT, LANES), F32)),
            ):
                left, right = halves(values[:, pair], spare, first)
                ref[rows, 2 * p * LANES : (2 * p + 1) * LANES] = left.astype(BF16)
                ref[rows, (2 * p + 1) * LANES : (2 * p + 2) * LANES] = right.astype(BF16)

    @pl.loop(0, row_len // QT)
    def _(t):
        rows = pl.ds(pl.multiple_of(t * QT, QT), QT)
        begin, number = reach(ends, live, t * QT, QT, row_len)

        @pl.when(number == 0)
        def _():
            o_ref[0, rows, :] = jnp.zeros((QT, D), BF16)

        for n in range(1, row_len // KG + 1):

            @pl.when(number == n)
            def _(n=n):
                span = pl.ds(pl.multiple_of(begin * KG, KG), n * KG)
                lane = lane_index(QT)

                @pl.loop(0, PAIRS)
                def _(p):
                    parts = []
                    for head in range(2):
                        cols = pl.ds(
                            pl.multiple_of((2 * p + head) * LANES, LANES), LANES
                        )
                        q = q_ref[0, rows, cols]
                        s = nt(q, kx[span, cols])
                        peak = jnp.max(s, axis=1, keepdims=True)
                        e = jnp.exp(s - peak).astype(BF16)
                        got = nn(e, vx[span, cols])
                        parts.append(got)
                        other = (lane >= DH) if head == 0 else (lane < DH)
                        total = peak + jnp.log(jnp.where(other, got, 1.0))
                        high, mid, rest = split_low(
                            jnp.where(peak > -0.5 * BIG, total, 0.0)
                        )
                        at = lane % DH
                        fill = jnp.where(
                            at == SAMP, -high, jnp.where(at == SAMP + 1, -mid, -rest)
                        )
                        spot = other & (at >= SAMP) & (at < SAMP + 3)
                        q_ref[0, rows, cols] = jnp.where(
                            spot, fill, q.astype(F32)
                        ).astype(BF16)
                    top = jnp.where(first, parts[0], parts[1])
                    total = pltpu.roll(jnp.where(first, parts[1], parts[0]), DH, 1)
                    cols = pl.ds(pl.multiple_of(p * LANES, LANES), LANES)
                    o_ref[0, rows, cols] = (top / total).astype(BF16)

    @pl.loop(0, row_len // QT)
    def _(t):
        rows = pl.ds(pl.multiple_of(t * QT, QT), QT)
        a1_ref[0, rows, :] = x_ref[0, rows, :].astype(F32) + (
            nn(o_ref[0, rows, :], w_ref[3]) + vec_ref[2:3, :]
        )


def attend(info, tokens, blocks, vec):
    micro, row_len, _ = tokens.shape
    row_spec = lambda width: pl.BlockSpec((1, row_len, width), lambda r: (r, 0, 0))
    return pl.pallas_call(
        attend_kernel,
        grid=(micro,),
        in_specs=[
            pl.BlockSpec(memory_space=pltpu.SMEM),
            row_spec(D),
            pl.BlockSpec((4, D, D), lambda r: (0, 0, 0)),
            pl.BlockSpec((NMAT, D), lambda r: (0, 0)),
        ],
        out_specs=[row_spec(D), row_spec(2 * D), row_spec(D), row_spec(D), row_spec(D)],
        out_shape=[
            jax.ShapeDtypeStruct((micro, row_len, D), F32),
            jax.ShapeDtypeStruct((micro, row_len, 2 * D), BF16),
            jax.ShapeDtypeStruct((micro, row_len, D), BF16),
            jax.ShapeDtypeStruct((micro, row_len, D), BF16),
            jax.ShapeDtypeStruct((micro, row_len, D), BF16),
        ],
        scratch_shapes=[
            pltpu.VMEM((row_len, 2 * D), BF16),
            pltpu.VMEM((row_len, 2 * D), BF16),
        ],
        compiler_params=pltpu.CompilerParams(vmem_limit_bytes=VMEM),
        cost_estimate=pl.CostEstimate(
            flops=micro * row_len * D * D * 8 + micro * H * row_len * row_len * DH * 4,
            bytes_accessed=micro * row_len * D * 16,
            transcendentals=micro * H * row_len * row_len,
        ),
    )(info, tokens, blocks, vec)


def gelu_both(u):
    t = 1.0 / (1.0 + (0.3275911 * 0.5**0.5) * jnp.abs(u))
    bell = jnp.exp(-0.5 * (u * u))
    tail = (
        t
        * (
            0.127414796
            + t * (-0.142248368 + t * (0.7107068705 + t * (-0.7265760135 + t * 0.5307027145)))
        )
        * bell
    )
    share = jnp.where(u >= 0, 1.0 - tail, tail)
    return u * share, share + u * bell * 0.3989422804014327


def norm_parts(a):
    center = a - jnp.mean(a, axis=-1, keepdims=True)
    rate = lax.rsqrt(jnp.mean(center * center, axis=-1, keepdims=True) + EPS)
    return center * rate, rate


def norm_back(grad, unit, rate):
    return rate * (
        grad
        - jnp.mean(grad, axis=-1, keepdims=True)
        - unit * jnp.mean(grad * unit, axis=-1, keepdims=True)
    )


def feed_kernel(
    info,
    a1_ref,
    w_ref,
    vec_ref,
    stu_ref,
    cls_ref,
    goal_ref,
    send_row,
    send_col,
    back_ref,
    da1_ref,
    out_ref,
    wg_ref,
    vg_ref,
    sg_ref,
    cg_ref,
    unit1,
    rate1,
    h1b,
    act,
    slope,
    unit2,
    rate2,
    zb,
    head_in,
    head_low,
    feed_low,
    *,
    tile,
    micro,
    row_len,
):
    step = pl.program_id(0)
    tiles = micro * row_len // tile
    group, _, slots, _ = out_ref.shape

    @pl.when(step == 0)
    def _():
        vg_ref[...] = jnp.zeros_like(vg_ref)

    @pl.when(step < tiles)
    def _():
        rows = pl.ds(pl.multiple_of(step * tile, tile), tile)
        unit, rate = norm_parts(a1_ref[...])
        unit1[rows, :] = unit
        rate1[rows, :] = rate
        h1 = unit * vec_ref[3:4, :] + vec_ref[4:5, :]
        low = h1.astype(BF16)
        h1b[rows, :] = low
        total = h1 + vec_ref[9:10, :]
        for c in range(FF // D):
            cols = slice(c * D, (c + 1) * D)
            value, grad = gelu_both(nn(low, w_ref[4 + c]) + vec_ref[5 + c : 6 + c, :])
            value = value.astype(BF16)
            act[rows, cols] = value
            slope[rows, cols] = grad.astype(BF16)
            total = total + nn(value, w_ref[8 + c])
        unit, rate = norm_parts(total)
        unit2[rows, :] = unit
        rate2[rows, :] = rate
        z = (unit * vec_ref[10:11, :] + vec_ref[11:12, :]).astype(BF16)
        zb[rows, :] = z
        head_in[rows, :] = nn(z, stu_ref[0:D, :].astype(BF16)) + stu_ref[D + SW : D + SW + 1, :]

    @pl.when(step == tiles)
    def _():
        head_phase(
            info, stu_ref, cls_ref, goal_ref, sg_ref, cg_ref, head_in, head_low, micro, row_len
        )
        sg_ref[0:D, :] = tn(zb[...], head_low[...])
        for m in range(micro):
            place = send_row[m : m + 1, :]
            spot = lax.broadcasted_iota(jnp.int32, (group * slots, row_len), 0)
            pick = jnp.where(spot == place, 1.0, 0.0).astype(BF16)
            moved = nn(pick, zb[m * row_len : (m + 1) * row_len, :]).astype(BF16)
            out_ref[:, m] = moved.reshape(group, slots, D)

    @pl.when(step >= tiles)
    def _():
        t = step - tiles
        rows = pl.ds(pl.multiple_of(t * tile, tile), tile)
        m = (t * tile) // row_len
        spot = lax.broadcasted_iota(jnp.int32, (tile, group * slots), 1)
        pick = jnp.where(spot == send_col[...], 1.0, 0.0).astype(BF16)
        dz = nn(pick, back_ref[:, m].reshape(group * slots, D))
        dz = dz + nt(head_low[rows, :], stu_ref[0:D, :].astype(BF16))
        unit = unit2[rows, :]
        vg_ref[10:11, :] += row_sum(dz * unit)
        vg_ref[11:12, :] += row_sum(dz)
        da2 = norm_back(dz * vec_ref[10:11, :], unit, rate2[rows, :])
        low = da2.astype(BF16)
        feed_low[rows, :] = low
        vg_ref[9:10, :] += row_sum(low.astype(F32))
        dh1 = da2
        for c in range(FF // D):
            cols = slice(c * D, (c + 1) * D)
            du = (nt(low, w_ref[8 + c]) * slope[rows, cols].astype(F32)).astype(BF16)
            slope[rows, cols] = du
            vg_ref[5 + c : 6 + c, :] += row_sum(du.astype(F32))
            dh1 = dh1 + nt(du, w_ref[4 + c])
        unit = unit1[rows, :]
        vg_ref[3:4, :] += row_sum(dh1 * unit)
        vg_ref[4:5, :] += row_sum(dh1)
        da1_ref[...] = norm_back(dh1 * vec_ref[3:4, :], unit, rate1[rows, :])

    @pl.when(step == 2 * tiles - 1)
    def _():
        for c in range(FF // D):
            cols = slice(c * D, (c + 1) * D)
            wg_ref[c] = tn(h1b[...], slope[:, cols]).astype(BF16)
            wg_ref[4 + c] = tn(act[:, cols], feed_low[...]).astype(BF16)


def head_phase(info, stu_ref, cls_ref, goal_ref, sg_ref, cg_ref, head_in, head_low, micro, row_len):
    scale = DH**-0.5
    query = stu_ref[D + SW + 2 : D + SW + 3, :]
    same = (
        lax.broadcasted_iota(jnp.int32, (SW, SW), 0) // DH
        == lax.broadcasted_iota(jnp.int32, (SW, SW), 1) // DH
    ).astype(F32)
    pooled, weights, members = [], [], []
    for m in range(micro):
        rows = slice(m * row_len, (m + 1) * row_len)
        s = head_in[rows, :]
        e = exact(s * query, same) * scale
        sample = sample_column(ends_of(info, m), 0, row_len)
        share = jnp.zeros_like(e)
        for j in range(SAMP):
            member = sample == j
            peak = jnp.max(jnp.where(member, e, -1e30), axis=0, keepdims=True)
            up = jnp.where(member, jnp.exp(jnp.where(member, e - peak, 0.0)), 0.0)
            up = up / row_sum(up)
            share = share + up
            pooled.append(row_sum(up * s))
            members.append(member)
        weights.append(share)
    pooled = jnp.concatenate(pooled, axis=0)
    pool_weight = stu_ref[D : D + SW, :]
    mixed = jnp.tanh(exact(pooled, pool_weight) + stu_ref[D + SW + 1 : D + SW + 2, :])
    classes = cls_ref[0:SW, :]
    logits = exact(mixed, classes) + cls_ref[SW : SW + 1, :]
    logits = logits - jnp.max(logits, axis=-1, keepdims=True)
    chance = jnp.exp(logits)
    chance = chance / jnp.sum(chance, axis=-1, keepdims=True)
    goal = goal_ref[:, 0:CLS]
    alive = goal_ref[:, CLS : CLS + 1]
    target = jnp.exp(goal - jnp.max(goal, axis=-1, keepdims=True))
    target = target / jnp.sum(target, axis=-1, keepdims=True)
    d_logits = alive * (chance - target)
    cg_ref[0:SW, :] = exact(mixed, d_logits, (((0,), (0,)), ((), ())))
    cg_ref[SW : SW + 1, :] = row_sum(d_logits)
    d_pre = exact(d_logits, classes, (((1,), (1,)), ((), ()))) * (1.0 - mixed * mixed)
    sg_ref[D : D + SW, :] = exact(pooled, d_pre, (((0,), (0,)), ((), ())))
    sg_ref[D + SW + 1 : D + SW + 2, :] = row_sum(d_pre)
    d_pooled = exact(d_pre, pool_weight, (((1,), (1,)), ((), ())))
    inner = exact(pooled * d_pooled, same)
    d_bias = jnp.zeros((1, SW), F32)
    d_query = jnp.zeros((1, SW), F32)
    for m in range(micro):
        rows = slice(m * row_len, (m + 1) * row_len)
        s = head_in[rows, :]
        spread = jnp.zeros((row_len, SW), F32)
        center = jnp.zeros((row_len, SW), F32)
        for j in range(SAMP):
            member = members[m * SAMP + j]
            at = m * SAMP + j
            spread = jnp.where(member, d_pooled[at : at + 1, :], spread)
            center = jnp.where(member, inner[at : at + 1, :], center)
        share = weights[m]
        d_e = share * (exact(s * spread, same) - center) * scale
        d_s = (share * spread + d_e * query).astype(BF16)
        head_low[rows, :] = d_s
        d_bias = d_bias + row_sum(d_s.astype(F32))
        d_query = d_query + row_sum(d_e * s)
    sg_ref[D + SW : D + SW + 1, :] = d_bias
    sg_ref[D + SW + 2 : D + SW + 3, :] = d_query


def feed(info, a1, blocks, vec, student, classifier, goals, send_row, send_col, returned):
    micro, row_len, _ = a1.shape
    tokens = micro * row_len
    tile = 256
    tiles = tokens // tile
    group, _, slots, _ = returned.shape
    whole = lambda *shape: pl.BlockSpec(shape, lambda i: (0,) * len(shape))
    once = lambda *shape: pl.BlockSpec(
        shape, lambda i: (0,) * len(shape), pipeline_mode=pl.Buffered(1)
    )
    ahead = lambda width: pl.BlockSpec((tile, width), lambda i: (jnp.minimum(i, tiles - 1), 0))
    behind = lambda width: pl.BlockSpec((tile, width), lambda i: (jnp.maximum(i - tiles, 0), 0))
    return pl.pallas_call(
        functools.partial(feed_kernel, tile=tile, micro=micro, row_len=row_len),
        grid=(2 * tiles,),
        in_specs=[
            pl.BlockSpec(memory_space=pltpu.SMEM),
            ahead(D),
            once(NMAT, D, D),
            once(NMAT, D),
            once(*student.shape),
            once(*classifier.shape),
            once(*goals.shape),
            once(*send_row.shape),
            behind(1),
            once(*returned.shape),
        ],
        out_specs=[
            behind(D),
            once(*returned.shape),
            once(8, D, D),
            once(NMAT, D),
            once(*student.shape),
            once(*classifier.shape),
        ],
        out_shape=[
            jax.ShapeDtypeStruct((tokens, D), F32),
            jax.ShapeDtypeStruct(returned.shape, BF16),
            jax.ShapeDtypeStruct((8, D, D), BF16),
            jax.ShapeDtypeStruct((NMAT, D), F32),
            jax.ShapeDtypeStruct(student.shape, F32),
            jax.ShapeDtypeStruct(classifier.shape, F32),
        ],
        scratch_shapes=[
            pltpu.VMEM((tokens, D), F32),
            pltpu.VMEM((tokens, 1), F32),
            pltpu.VMEM((tokens, D), BF16),
            pltpu.VMEM((tokens, FF), BF16),
            pltpu.VMEM((tokens, FF), BF16),
            pltpu.VMEM((tokens, D), F32),
            pltpu.VMEM((tokens, 1), F32),
            pltpu.VMEM((tokens, D), BF16),
            pltpu.VMEM((tokens, SW), F32),
            pltpu.VMEM((tokens, SW), BF16),
            pltpu.VMEM((tokens, D), BF16),
        ],
        compiler_params=pltpu.CompilerParams(vmem_limit_bytes=VMEM),
        cost_estimate=pl.CostEstimate(
            flops=tokens * D * FF * 12, bytes_accessed=tokens * D * 16, transcendentals=tokens * FF
        ),
    )(
        info,
        a1.reshape(tokens, D),
        blocks,
        vec,
        student,
        classifier,
        goals,
        send_row,
        send_col,
        returned,
    )


def attend_back_kernel(
    info,
    x_ref,
    da1_ref,
    q_ref,
    k_ref,
    v_ref,
    o_ref,
    w_ref,
    dx_ref,
    wg_ref,
    vg_ref,
    kx,
    vx,
    dox,
    dq,
    dk,
    dv,
    wsum,
    *,
    micro,
):
    row = pl.program_id(0)
    row_len = x_ref.shape[1]
    ends, live = ends_of(info, row), live_of(info, row)
    first = lane_index(QT) < DH

    @pl.when(row == 0)
    def _():
        vg_ref[...] = jnp.zeros_like(vg_ref)
        wsum[...] = jnp.zeros_like(wsum)

    crossed = (
        lax.broadcasted_iota(jnp.int32, (LANES, LANES), 0) // DH
        != lax.broadcasted_iota(jnp.int32, (LANES, LANES), 1) // DH
    )
    crossed = jnp.where(crossed, 1.0, 0.0).astype(BF16)

    dq[...] = jnp.zeros_like(dq)

    @pl.loop(0, row_len // QT)
    def _(t):
        rows = pl.ds(pl.multiple_of(t * QT, QT), QT)
        sample = sample_column(ends, t * QT, QT)
        k_extra = key_spare(sample, QT)
        branch = da1_ref[0, rows, :].astype(BF16)
        vg_ref[2:3, :] += row_sum(branch.astype(F32))
        do = nt(branch, w_ref[3]).astype(BF16).astype(F32)
        inner = do * o_ref[0, rows, :].astype(F32)
        lane = lane_index(QT) % DH
        for p in range(PAIRS):
            pair = slice(p * LANES, (p + 1) * LANES)
            high = inner[:, pair].astype(BF16)
            rest = (inner[:, pair] - high.astype(F32)).astype(BF16)
            delta = nn(high, crossed) + nn(rest, crossed)
            high, mid, _rest = split_low(delta)
            do_extra = jnp.where(lane == 0, -high, jnp.where(lane == 1, -mid, 0.0))
            for ref, values, spare in (
                (dox, do[:, pair], do_extra),
                (kx, k_ref[0, rows, pair].astype(F32), k_extra),
                (vx, v_ref[0, rows, pair].astype(F32), jnp.ones((QT, LANES), F32)),
            ):
                left, right = halves(values, spare, first)
                ref[rows, 2 * p * LANES : (2 * p + 1) * LANES] = left.astype(BF16)
                ref[rows, (2 * p + 1) * LANES : (2 * p + 2) * LANES] = right.astype(BF16)

    @pl.loop(0, row_len // QT)
    def _(t):
        rows = pl.ds(pl.multiple_of(t * QT, QT), QT)
        begin, number = reach(ends, live, t * QT, QT, row_len)

        @pl.when(number == 0)
        def _():
            dk[rows, :] = jnp.zeros((QT, D), BF16)
            dv[rows, :] = jnp.zeros((QT, D), BF16)

        for n in range(1, row_len // KG + 1):

            @pl.when(number == n)
            def _(n=n):
                span = pl.ds(pl.multiple_of(begin * KG, KG), n * KG)
                wide = lane_index(n * KG) < DH

                @pl.loop(0, PAIRS)
                def _(p):
                    got = []
                    for head in range(2):
                        cols = pl.ds(
                            pl.multiple_of((2 * p + head) * LANES, LANES), LANES
                        )
                        q, k = q_ref[0, span, cols], kx[rows, cols]
                        do = dox[span, cols]
                        prob = jnp.exp(nt(k, q))
                        ds = (prob * nt(vx[rows, cols], do)).astype(BF16)
                        got.append(
                            (nn(prob.astype(BF16), do), nn(ds, q), tn(ds, k))
                        )
                    cols = pl.ds(pl.multiple_of(p * LANES, LANES), LANES)
                    dv[rows, cols] = jnp.where(first, got[0][0], got[1][0]).astype(BF16)
                    dk[rows, cols] = jnp.where(first, got[0][1], got[1][1]).astype(BF16)
                    dq[span, cols] += jnp.where(wide, got[0][2], got[1][2])

    @pl.loop(0, row_len // QT)
    def _(t):
        rows = pl.ds(pl.multiple_of(t * QT, QT), QT)
        dq_low = (dq[rows, :] * DH**-0.5).astype(BF16)
        dk_low, dv_low = dk[rows, :], dv[rows, :]
        vg_ref[0:1, :] += row_sum(dq_low.astype(F32))
        vg_ref[1:2, :] += row_sum(dv_low.astype(F32))
        dx_ref[0, rows, :] = (
            da1_ref[0, rows, :]
            + nt(dq_low, w_ref[0])
            + nt(dk_low, w_ref[1])
            + nt(dv_low, w_ref[2])
        ).astype(BF16)

    x = x_ref[0]
    wsum[0] += tn(x, (dq[...] * DH**-0.5).astype(BF16))
    wsum[1] += tn(x, dk[...])
    wsum[2] += tn(x, dv[...])
    wsum[3] += tn(o_ref[0], da1_ref[0].astype(BF16))

    @pl.when(row == micro - 1)
    def _():
        wg_ref[...] = wsum[...].astype(BF16)


def attend_back(info, tokens, da1, q, k, v, o, blocks):
    micro, row_len, _ = tokens.shape
    row_spec = lambda width: pl.BlockSpec((1, row_len, width), lambda r: (r, 0, 0))
    return pl.pallas_call(
        functools.partial(attend_back_kernel, micro=micro),
        grid=(micro,),
        in_specs=[
            pl.BlockSpec(memory_space=pltpu.SMEM),
            row_spec(D),
            row_spec(D),
            row_spec(2 * D),
            row_spec(D),
            row_spec(D),
            row_spec(D),
            pl.BlockSpec((4, D, D), lambda r: (0, 0, 0)),
        ],
        out_specs=[
            row_spec(D),
            pl.BlockSpec((4, D, D), lambda r: (0, 0, 0)),
            pl.BlockSpec((8, D), lambda r: (0, 0)),
        ],
        out_shape=[
            jax.ShapeDtypeStruct((micro, row_len, D), BF16),
            jax.ShapeDtypeStruct((4, D, D), BF16),
            jax.ShapeDtypeStruct((8, D), F32),
        ],
        scratch_shapes=[
            pltpu.VMEM((row_len, 2 * D), BF16),
            pltpu.VMEM((row_len, 2 * D), BF16),
            pltpu.VMEM((row_len, 2 * D), BF16),
            pltpu.VMEM((row_len, D), F32),
            pltpu.VMEM((row_len, D), BF16),
            pltpu.VMEM((row_len, D), BF16),
            pltpu.VMEM((4, D, D), F32),
        ],
        compiler_params=pltpu.CompilerParams(vmem_limit_bytes=VMEM),
        cost_estimate=pl.CostEstimate(
            flops=micro * row_len * D * D * 16 + micro * H * row_len * row_len * DH * 10,
            bytes_accessed=micro * row_len * D * 16,
            transcendentals=micro * H * row_len * row_len,
        ),
    )(info, tokens, da1, q, k, v, o, blocks)


def pick_kernel(place_ref, rows_ref, out_ref):
    group, _, slots, _ = out_ref.shape
    places = group * slots
    spot = lax.broadcasted_iota(jnp.int32, (places, rows_ref.shape[1]), 1)
    pick = jnp.where(spot == place_ref[0], 1.0, 0.0).astype(BF16)
    out_ref[:, 0] = nn(pick, rows_ref[0]).astype(BF16).reshape(group, slots, D)


def pick_rows(place_col, rows, group):
    micro, row_len, _ = rows.shape
    slots = row_len // group
    return pl.pallas_call(
        pick_kernel,
        grid=(micro,),
        in_specs=[
            pl.BlockSpec((1, row_len, 1), lambda m: (m, 0, 0)),
            pl.BlockSpec((1, row_len, D), lambda m: (m, 0, 0)),
        ],
        out_specs=pl.BlockSpec((group, 1, slots, D), lambda m: (0, m, 0, 0)),
        out_shape=jax.ShapeDtypeStruct((group, micro, slots, D), BF16),
        compiler_params=pltpu.CompilerParams(vmem_limit_bytes=VMEM),
    )(place_col, rows)


def place_kernel(place_ref, rows_ref, out_ref):
    row_len = out_ref.shape[1]
    spot = lax.broadcasted_iota(jnp.int32, (row_len, row_len), 0)
    pick = jnp.where(spot == place_ref[0], 1.0, 0.0).astype(BF16)
    out_ref[0] = nn(pick, rows_ref[:, 0].reshape(row_len, D)).astype(BF16)


def place_rows(place_row, rows):
    group, micro, slots, _ = rows.shape
    row_len = group * slots
    return pl.pallas_call(
        place_kernel,
        grid=(micro,),
        in_specs=[
            pl.BlockSpec((1, 1, row_len), lambda m: (m, 0, 0)),
            pl.BlockSpec((group, 1, slots, D), lambda m: (0, m, 0, 0)),
        ],
        out_specs=pl.BlockSpec((1, row_len, D), lambda m: (m, 0, 0)),
        out_shape=jax.ShapeDtypeStruct((micro, row_len, D), BF16),
        compiler_params=pltpu.CompilerParams(vmem_limit_bytes=VMEM),
    )(place_row, rows)


def diagonal_rule(old_values, moment, grads, rate):
    new_moment = decay_rate * moment + (1.0 - decay_rate) * grads * grads
    return (new_moment, old_values - rate * grads / (jnp.sqrt(new_moment) + 1e-08))


def local(
    tokens,
    cotangent,
    lengths,
    exit_layers,
    teacher,
    blocks,
    left_stats,
    right_stats,
    left_root,
    right_root,
    vectors,
    vec_moment,
    student,
    stu_moment,
    classifier,
    cls_moment,
):
    group = lax.axis_size("batch")
    me = lax.axis_index("batch")
    micro, _, row_len, _ = tokens.shape
    slots = row_len // group
    tokens, cotangent = tokens[:, 0], cotangent[:, 0]
    ends = jnp.cumsum(lengths[:, 0], axis=-1, dtype=jnp.int32)
    live = (exit_layers[:, 0] >= LAYER).astype(jnp.int32)
    info = jnp.concatenate([ends, live], axis=1)
    alive_len = lengths[:, 0] * live
    counts = jnp.sum(alive_len, axis=1, dtype=jnp.int32)
    everyone = lax.all_gather(counts[None, :], "batch", axis=0, tiled=True)
    starts = jnp.cumsum(everyone, axis=0, dtype=jnp.int32) - everyone

    places = jnp.arange(row_len, dtype=jnp.int32)
    before = jnp.cumsum(alive_len, axis=1, dtype=jnp.int32) - alive_len
    sample = jnp.sum((places[None, :, None] >= ends[:, None, : SAMP - 1]).astype(jnp.int32), axis=-1)
    chosen = sample[..., None] == jnp.arange(SAMP, dtype=jnp.int32)
    shift = jnp.sum(jnp.where(chosen, (before - ends + lengths[:, 0])[:, None, :], 0), axis=-1)
    alive_tok = jnp.sum(jnp.where(chosen, live[:, None, :], 0), axis=-1)
    rank = places[None, :] + shift
    send = (starts[me][:, None] + rank) % group * slots + rank // group
    send = jnp.where(alive_tok > 0, send, row_len)
    start_of = jnp.repeat(starts.T, slots, axis=1)
    count_of = jnp.repeat(everyone.T, slots, axis=1)
    turn = (me - start_of) % group + group * (places % slots)[None, :]
    back = jnp.where(turn < count_of, (start_of + turn) // group, row_len)

    grad_outgoing = pick_rows(back[:, :, None], cotangent, group)
    returned = lax.all_to_all(grad_outgoing, "batch", split_axis=0, concat_axis=0, tiled=True)

    matrices = lax.all_gather(blocks, "shard", axis=0, tiled=True)
    vec = lax.all_gather(vectors.astype(BF16), "shard", axis=0, tiled=True).astype(F32)

    a1, q, k, v, o = attend(info, tokens, matrices, vec)
    goals = jnp.concatenate(
        [teacher[:, 0], live[..., None].astype(F32)], axis=-1
    ).reshape(micro * SAMP, CLS + 1)
    da1, outgoing, ff_grads, ff_vecs, stu_grads, cls_grads = feed(
        info, a1, matrices, vec, student, classifier, goals, send, send.reshape(-1, 1), returned
    )
    arrived = lax.all_to_all(outgoing, "batch", split_axis=0, concat_axis=0, tiled=True)
    input_grads, at_grads, at_vecs = attend_back(
        info, tokens, da1.reshape(micro, row_len, D), q, k, v, o, matrices
    )
    layer_out = place_rows(back[:, None, :], arrived)

    grads = jnp.concatenate([at_grads, ff_grads], axis=0)
    vec_grads = jnp.concatenate([at_vecs[:3], ff_vecs[3:]], axis=0)
    owned = lax.psum_scatter(grads, "shard", scatter_dimension=0, tiled=True)
    owned = lax.psum(owned, "batch")
    small = jnp.concatenate(
        [vec_grads.reshape(-1), stu_grads.reshape(-1), cls_grads.reshape(-1)]
    )
    small = lax.psum(small, ("batch", "shard"))
    whole_vecs = small[: NMAT * D].reshape(NMAT, D)
    head_student = small[NMAT * D : NMAT * D + student.size].reshape(student.shape)
    head_class = small[NMAT * D + student.size :].reshape(classifier.shape)
    owners = lax.axis_size("shard")
    owned_vecs = lax.dynamic_slice_in_dim(
        whole_vecs, lax.axis_index("shard") * (NMAT // owners), NMAT // owners, 0
    )

    owned_f32 = owned.astype(F32)
    gram_left = jnp.einsum("bij,bkj->bik", owned, owned, preferred_element_type=F32)
    gram_right = jnp.einsum("bji,bjk->bik", owned, owned, preferred_element_type=F32)
    new_left = decay_rate * left_stats + (1.0 - decay_rate) * gram_left
    new_right = decay_rate * right_stats + (1.0 - decay_rate) * gram_right
    steered = jnp.einsum("bij,bjk->bik", left_root, owned_f32)
    steered = jnp.einsum("bij,bjk->bik", steered, right_root)
    size_norm = jnp.sqrt(jnp.mean(steered * steered, axis=(1, 2), keepdims=True) + 1e-06)
    new_blocks = blocks.astype(F32) - block_rate * steered / size_norm
    new_vec_moment, new_vectors = diagonal_rule(vectors, vec_moment, owned_vecs, vector_rate)
    new_stu_moment, new_student = diagonal_rule(student, stu_moment, head_student, head_rate)
    new_cls_moment, new_classifier = diagonal_rule(classifier, cls_moment, head_class, head_rate)
    return (
        layer_out[:, None],
        input_grads[:, None],
        owned_f32,
        new_blocks,
        new_left,
        new_right,
        owned_vecs,
        new_vec_moment,
        new_vectors,
        head_student,
        new_stu_moment,
        new_student,
        head_class,
        new_cls_moment,
        new_classifier,
    )


def solution(mesh):
    rows = P(None, ("batch", "shard"), None, None)
    tags = P(None, ("batch", "shard"), None)
    mats = P("shard", None, None)
    vecs = P("shard", None)
    return jax.shard_map(
        local,
        mesh=mesh,
        in_specs=(rows, rows, tags, tags, rows, mats, mats, mats, mats, mats, vecs, vecs)
        + (P(),) * 4,
        out_specs=(rows, rows, mats, mats, mats, mats, vecs, vecs, vecs) + (P(),) * 6,
        check_vma=False,
    )
```

time: 1390 us -> 576 us (0.41); the launches traced: 1380 us -> 579 us
  blocking collectives: 559 us -> 18.7 us
  matrix products: 370 us -> 11.2 us
  waiting for transfers between devices: 9.08 us -> 271 us
  local copies, waits for them, and re-layouts: 249 us -> 14.8 us
  Pallas kernels: 0 us -> 173 us
  other arithmetic: 156 us -> 31.4 us
  starting transfers between devices: 17.7 us -> 44.5 us
    psum x2 -> x0, blocking collectives: 529 us -> none  [the longest x1 489 us: local(): whole_blocks, whole_vectors = lax.psum((grad_blocks, grad_vectors), 'batch')]
    dot_general x80 -> x3, matrix products: 370 us -> 11.2 us  [the longest x1 5.83 us: local(): steered = jnp.einsum('bij,bjk->bik', steered, right_root)]
    psum x1 -> x2, waiting for transfers between devices: 0.01 us -> 214 us  [the longest x1 133 us: local(): small = lax.psum(small, ('batch', 'shard'))]
    pallas_call x0 -> x5, Pallas kernels: none -> 173 us  [the longest x1 86.1 us: feed(): pl.pallas_call(functools.partial(feed_kernel, tile=tile, micro=micro, row...]
    convert_element_type x8 -> x2, other arithmetic: 61.7 us -> 2.1 us  [the longest x1 2.1 us: local(): owned_f32 = owned.astype(F32)]
    reduce_scatter x1, waiting for transfers between devices: 0.01 us -> 56.2 us  [local(): owned = lax.psum_scatter(grads, 'shard', scatter_dimension=0, tiled=True)]
    gather x8 -> x0, local copies, waits for them, and re-layouts: 43.4 us -> none  [the longest x4 17.5 us: local(): grad_normed = grad_normed + returned_rows[send_index].astype(jnp.float32)]
    reduce_sum x34 -> x3, other arithmetic: 43.3 us -> 1 us  [the longest x1 0.79 us: local(): counts = jnp.sum(alive_len, axis=1, dtype=jnp.int32)]
  transfers between devices with their start and end apart: 7 -> 6, of which waited for: 3 -> 3; matrix products, arithmetic and copies ran while one was open for 11% -> 6% of each run, Pallas kernels for 0% -> 7%
where the time goes in v1:
time: 576 us; the launch traced here: 579 us
  waiting for transfers between devices  271 us (47%)
  Pallas kernels  173 us (30%)
  starting transfers between devices  44.5 us (8%)
  other arithmetic  31.4 us (5%)
  blocking collectives  18.7 us (3%)
  between operations  14.9 us (3%)
  local copies, waits for them, and re-layouts  14.8 us (3%)
  matrix products  11.2 us (2%)
    psum x1, waiting for transfers between devices, local(): small = lax.psum(small, ('batch', 'shard'))  133 us
    pallas_call x1, Pallas kernels, feed(): pl.pallas_call(functools.partial(feed_kernel, tile=tile, micro=micro, row...  86.1 us
    psum x1, waiting for transfers between devices, local(): owned = lax.psum(owned, 'batch')  81.2 us
    reduce_scatter x1, waiting for transfers between devices, local(): owned = lax.psum_scatter(grads, 'shard', scatter_dimension=0, tiled=True)  56.2 us
    pallas_call x1, Pallas kernels, attend_back(): pl.pallas_call(functools.partial(attend_back_kernel, micro=micro), grid=(...  44.5 us
    all_to_all x1, starting transfers between devices, local(): lax.all_to_all(outgoing, 'batch', split_axis=0, concat_axis=0, tiled=True)  39.9 us
    pallas_call x1, Pallas kernels, attend(): pl.pallas_call(attend_kernel, grid=(micro,), in_specs=[pl.BlockSpec(memor...  32.8 us
    unnamed x1, blocking collectives  13.1 us
  transfers between devices with their start and end apart: 6, of which 3 were waited for; matrix products, arithmetic and copies ran while one was open for 6% of the time, Pallas kernels for 7%

profile of v1, /device:TPU:0, one launch (start us, length us, event | category | flops | bytes accessed | tf_op | source)
XLA Modules:
  0.0 579.2 jit_solution(10162040278829200033)
XLA Ops:
  7.9 1.4 dynamic-slice
  10.7 0.8 fusion.31
  11.8 13.1 %all-reduce = s32[16]{0:T(128)S(1)} all-reduce(s32[16]{0:T(128)S(1)} %dynamic-update-slice), channel_id=2, replica_groups=mesh['batch'=8,'shard'=4] {'batch'}, use_global_device_ids=true, to_apply=%add | all-reduce | flops 16 | bytes 128
  25.2 1.9 reshape.533
  27.1 1.8 reshape.534
  28.9 3.7 fusion.11.place_ref
  32.6 5.0 shard_map.272
  37.6 4.5 all-to-all-start
  43.7 5.6 all-gather.1
  51.1 1.3 copy.154
  52.5 1.3 copy.156
  55.1 3.7 fusion.6.send_col
  58.8 32.8 %shard_map.271 = (f32[2,1024,512]{2,1,0:T(8,128)}, bf16[2,1024,1024]{2,1,0:T(8,128)(2,1)}, bf16[2,1024,512]{2,1,0:T(8,128)(2,1)}, bf16[2,1024,512]{2,1,0:T(8,128)(2,1)}, bf16[2,1024,512]{2,1,0:T(8,128)(2,1)}) custom-call(s32[2,8]{1,0:T(2,128)} %pad_add_fusion.info, bf16[2,1024,512]{2,1,0:T(8,128)(2,1)} %bitcast.107, ...), custom_call_target="tpu_custom_call" | custom-call | flops 8589934592 | bytes 16777216 | tf_op jit(solution)/shard_map/pallas_call | solution.py:204
  91.6 86.1 %shard_map.273 = (f32[2048,512]{1,0:T(8,128)}, bf16[8,2,128,512]{3,2,1,0:T(8,128)(2,1)}, bf16[8,512,512]{2,1,0:T(8,128)(2,1)}, f32[12,512]{1,0:T(8,128)}, f32[643,128]{1,0:T(8,128)}, /*index=5*/f32[129,14]{1,0:T(8,128)}) custom-call(s32[2,8]{1,0:T(2,128)} %pad_add_fusion.info, f32[2048,512]{1,0:T(8,128)} %bitcast.109, ...), custom_call_target="tpu_custom_call" | custom-call | flops 25769803776 | bytes 16777216 | tf_op jit(solution)/shard_map/pallas_call | solution.py:454
  177.7 44.5 %shard_map.275 = (bf16[2,1024,512]{2,1,0:T(8,128)(2,1)}, bf16[4,512,512]{2,1,0:T(8,128)(2,1)}, f32[8,512]{1,0:T(8,128)}) custom-call(s32[2,8]{1,0:T(2,128)} %pad_add_fusion.info, bf16[2,1024,512]{2,1,0:T(8,128)(2,1)} %bitcast.108, f32[2,1024,512]{2,1,0:T(8,128)} %bitcast.110, bf16[2,1024,1024]{2,1,0:T(8,128)(2,1)} %get-tuple-element.32.q_ref, ...), custom_call_target="tpu_custom_call" | custom-call | flops 19327352832 | bytes 16777216 | tf_op jit(solution)/shard_map/pallas_call | solution.py:646
  222.3 6.1 %pad_maximum_fusion = bf16[12,512,512]{2,1,0:T(8,128)(2,1)} fusion(bf16[8,512,512]{2,1,0:T(8,128)(2,1)} %get-tuple-element.38, bf16[4,512,512]{2,1,0:T(8,128)(2,1)} %get-tuple-element.37), kind=kLoop, calls=%fused_computation | loop fusion | flops 3145728 | bytes 12582912 | tf_op jit(solution)/shard_map/concatenate | solution.py:803
  228.4 39.9 %all-to-all-start.1 = ((bf16[8,2,128,512]{3,2,1,0:T(8,128)(2,1)}), bf16[8,2,128,512]{3,2,1,0:T(8,128)(2,1)}, u32[]{:S(2)}, u32[]{:S(2)}) async-start(bf16[8,2,128,512]{3,2,1,0:T(8,128)(2,1)} %get-tuple-element.30), calls=%async_computation.1 | async-start | bytes 4194304 | tf_op jit(solution)/shard_map/all_to_all | solution.py:797
  268.3 1.6 reshape.520
  270.0 1.5 pad_maximum_fusion.1
  271.5 56.2 %reduce-scatter.2.cloned.1.call-done = bf16[3,512,512]{2,1,0:T(8,128)(2,1)} async-done(((bf16[12,512,512]{2,1,0:T(8,128)(2,1)}), bf16[3,512,512]{2,1,0:T(8,128)(2,1)}) %reduce-scatter.2.cloned.1.call-update) | async-done | bytes 1572880 | tf_op jit(solution)/shard_map/reduce_scatter | solution.py:805
  328.5 132.5 %all-reduce.6.cloned.1.call-done = f32[90254]{0:T(1024)} async-done(((f32[90254]{0:T(1024)}), f32[90254]{0:T(1024)}) %all-reduce.6.cloned.1.call-update) | async-done | bytes 361032 | tf_op jit(solution)/shard_map/psum | solution.py:810
  462.7 1.4 divide_subtract_fusion.3
  464.0 1.4 divide_subtract_fusion.2
  465.4 2.2 divide_subtract_fusion.1
  467.6 4.7 shard_map.274
  472.3 81.2 %all-reduce.4.cloned.1.call-done = bf16[3,512,512]{2,1,0:T(8,128)(2,1)} async-done(((bf16[3,512,512]{2,1,0:T(8,128)(2,1)}), bf16[3,512,512]{2,1,0:T(8,128)(2,1)}) %all-reduce.4.cloned.1.call-update) | async-done | bytes 1572880 | tf_op jit(solution)/shard_map/psum | solution.py:806
  553.5 5.8 %multiply_reduce_fusion = (f32[3]{0:T(128)S(1)}, f32[3,512,512]{2,1,0:T(8,128)}) fusion(f32[3,512,512]{2,1,0:T(8,128)S(1)} %copy-done, bf16[3,512,512]{2,1,0:T(8,128)(2,1)} %all-reduce.4.cloned.1.call-done, f32[3,512,512]{2,1,0:T(8,128)} %param.24), kind=kOutput, calls=%fused_computation.4 | convolution fusion | flops 1612185600 | bytes 11010060 | tf_op jit(solution)/shard_map/bij,bjk->bik/dot_general | solution.py:825
  559.3 4.8 divide_subtract_fusion
  564.1 2.1 convert_element_type.52
  566.2 0.9 copy-done.2
  567.1 2.7 add_multiply_fusion
  569.8 2.7 add_multiply_fusion.1
  (76 shorter events, 9.3 us)
Async XLA Ops:
  7.2 546.3 %copy-start = (f32[3,512,512]{2,1,0:T(8,128)S(1)}, f32[3,512,512]{2,1,0:T(8,128)}, u32[]{:S(2)}) copy-start(f32[3,512,512]{2,1,0:T(8,128)} %param.25) | copy-start | bytes 9437188
  7.2 51.6 %all-gather.4.cloned.1.call-start = ((), (), s32[]{:S(2)}) async-start(), calls=%async_computation.3 | async-start | bytes 7864320 | tf_op jit(solution)/shard_map/all_gather | solution.py:787
  37.6 4.6 copy-start.9
  37.6 6.1 %copy-start.7 = (f32[3,512]{1,0:T(4,128)S(1)}, f32[3,512]{1,0:T(4,128)}, u32[]{:S(2)}) copy-start(f32[3,512]{1,0:T(4,128)} %param.26) | copy-start | bytes 18436
  37.6 12.4 %copy-start.5 = (f32[129,14]{0,1:T(8,128)S(1)}, f32[129,14]{0,1:T(8,128)}, u32[]{:S(2)}) copy-start(f32[129,14]{0,1:T(8,128)} %param.30) | copy-start | bytes 21676
  37.6 16.9 %copy-start.10 = (f32[2,1,4,14]{3,2,1,0:T(4,128)S(1)}, f32[2,1,4,14]{3,2,1,0:T(4,128)}, u32[]{:S(2)}) copy-start(f32[2,1,4,14]{3,2,1,0:T(4,128)} %param.20) | copy-start | bytes 1348
  37.6 54.0 %all-to-all-start = ((bf16[8,2,128,512]{3,2,1,0:T(8,128)(2,1)}), bf16[8,2,128,512]{3,2,1,0:T(8,128)(2,1)}, u32[]{:S(2)}, u32[]{:S(2)}) async-start(bf16[8,2,128,512]{3,2,1,0:T(8,128)(2,1)} %shard_map.272), calls=%async_computation | async-start | bytes 4194304 | tf_op jit(solution)/shard_map/all_to_all | solution.py:785
  42.1 285.7 %reduce-scatter.2.cloned.1.call-start = ((), (), s32[]{:S(2)}) async-start(), calls=%async_computation.4 | async-start | bytes 7864320 | tf_op jit(solution)/shard_map/reduce_scatter | solution.py:805
  228.3 39.9 %copy-start.11 = (f32[8,512]{1,0:T(8,128)S(1)}, f32[8,512]{1,0:T(8,128)}, u32[]{:S(2)}) copy-start(f32[8,512]{1,0:T(8,128)} %get-tuple-element.39) | copy-start | bytes 49156
  228.4 41.6 %copy-start.8 = (f32[12,512]{1,0:T(8,128)S(1)}, f32[12,512]{1,0:T(8,128)}, u32[]{:S(2)}) copy-start(f32[12,512]{1,0:T(8,128)} %get-tuple-element.40) | copy-start | bytes 73732
  228.4 41.6 %copy-start.4 = (f32[643,128]{1,0:T(8,128)S(1)}, f32[643,128]{1,0:T(8,128)}, u32[]{:S(2)}) copy-start(f32[643,128]{1,0:T(8,128)} %get-tuple-element.41) | copy-start | bytes 987652
  228.4 239.2 %all-to-all-start.1 = ((bf16[8,2,128,512]{3,2,1,0:T(8,128)(2,1)}), bf16[8,2,128,512]{3,2,1,0:T(8,128)(2,1)}, u32[]{:S(2)}, u32[]{:S(2)}) async-start(bf16[8,2,128,512]{3,2,1,0:T(8,128)(2,1)} %get-tuple-element.30), calls=%async_computation.1 | async-start | bytes 4194304 | tf_op jit(solution)/shard_map/all_to_all | solution.py:797
  268.2 192.8 %all-reduce.6.cloned.1.call-start = ((), (), s32[]{:S(2)}) async-start(), calls=%async_computation.6 | async-start | bytes 729088 | tf_op jit(solution)/shard_map/psum | solution.py:810
  271.5 282.0 %all-reduce.4.cloned.1.call-start = ((), (), s32[]{:S(2)}) async-start(), calls=%async_computation.5 | async-start | bytes 3145728 | tf_op jit(solution)/shard_map/psum | solution.py:806
  462.7 9.6 %copy-start.6 = (f32[129,14]{0,1:T(8,128)}, f32[129,14]{0,1:T(8,128)S(1)}, u32[]{:S(2)}) copy-start(f32[129,14]{0,1:T(8,128)S(1)} %copy.147) | copy-start | bytes 21676
  559.3 4.8 copy-start.1
  564.1 3.0 copy-start.2
  567.1 2.7 copy-start.3
Sparse Core Ops, SparseCore 0:
  9.6 49.1 all-gather.3
  228.5 99.2 reduce-scatter.1
  334.6 126.3 all-reduce.5
  464.4 89.0 all-reduce.3

commit v2 on v1

--- a/solution.py
+++ b/solution.py
@@ -477,7 +477,7 @@
         out_shape=[
             jax.ShapeDtypeStruct((tokens, D), F32),
             jax.ShapeDtypeStruct(returned.shape, BF16),
-            jax.ShapeDtypeStruct((8, D, D), BF16),
+            jax.ShapeDtypeStruct((NMAT, D, D), BF16),
             jax.ShapeDtypeStruct((NMAT, D), F32),
             jax.ShapeDtypeStruct(student.shape, F32),
             jax.ShapeDtypeStruct(classifier.shape, F32),
@@ -522,6 +522,7 @@
     v_ref,
     o_ref,
     w_ref,
+    _,
     dx_ref,
     wg_ref,
     vg_ref,
@@ -640,7 +641,7 @@
         wg_ref[...] = wsum[...].astype(BF16)
 
 
-def attend_back(info, tokens, da1, q, k, v, o, blocks):
+def attend_back(info, tokens, da1, q, k, v, o, blocks, grads):
     micro, row_len, _ = tokens.shape
     row_spec = lambda width: pl.BlockSpec((1, row_len, width), lambda r: (r, 0, 0))
     return pl.pallas_call(
@@ -655,15 +656,16 @@
             row_spec(D),
             row_spec(D),
             pl.BlockSpec((4, D, D), lambda r: (0, 0, 0)),
+            pl.BlockSpec(memory_space=pl.ANY),
         ],
         out_specs=[
             row_spec(D),
-            pl.BlockSpec((4, D, D), lambda r: (0, 0, 0)),
+            pl.BlockSpec((4, D, D), lambda r: (2, 0, 0)),
             pl.BlockSpec((8, D), lambda r: (0, 0)),
         ],
         out_shape=[
             jax.ShapeDtypeStruct((micro, row_len, D), BF16),
-            jax.ShapeDtypeStruct((4, D, D), BF16),
+            jax.ShapeDtypeStruct((NMAT, D, D), BF16),
             jax.ShapeDtypeStruct((8, D), F32),
         ],
         scratch_shapes=[
@@ -675,13 +677,14 @@
             pltpu.VMEM((row_len, D), BF16),
             pltpu.VMEM((4, D, D), F32),
         ],
+        input_output_aliases={8: 1},
         compiler_params=pltpu.CompilerParams(vmem_limit_bytes=VMEM),
         cost_estimate=pl.CostEstimate(
             flops=micro * row_len * D * D * 16 + micro * H * row_len * row_len * DH * 10,
             bytes_accessed=micro * row_len * D * 16,
             transcendentals=micro * H * row_len * row_len,
         ),
-    )(info, tokens, da1, q, k, v, o, blocks)
+    )(info, tokens, da1, q, k, v, o, blocks, grads)
 
 
 def pick_kernel(place_ref, rows_ref, out_ref):
@@ -731,9 +734,381 @@
     )(place_row, rows)
 
 
-def diagonal_rule(old_values, moment, grads, rate):
-    new_moment = decay_rate * moment + (1.0 - decay_rate) * grads * grads
-    return (new_moment, old_values - rate * grads / (jnp.sqrt(new_moment) + 1e-08))
+CHUNKS = 6
+STU_ROWS, CLS_ROWS, VEC_ROWS = 656, 144, 16
+SMALL_ROWS = STU_ROWS + CLS_ROWS + 4 * VEC_ROWS
+
+
+def bits_of(size):
+    return [1 << i for i in range(size.bit_length() - 1)]
+
+
+def reduce_kernel(
+    group,
+    owners,
+    grad_ref,
+    ff_vec,
+    at_vec,
+    stu_ref,
+    cls_ref,
+    own_ref,
+    vec_out,
+    stu_out,
+    cls_out,
+    got_a,
+    sum_a,
+    got_b,
+    part,
+    got_c,
+    final,
+    small,
+    small_got,
+    small_sum,
+    small_end,
+    send_sem,
+    recv_sem,
+    small_send,
+    small_recv,
+):
+    b, s = lax.axis_index("batch"), lax.axis_index("shard")
+    per = NMAT // owners
+    rows = per * D // CHUNKS
+    batch_bits, shard_bits = bits_of(group), bits_of(owners)
+    half = SMALL_ROWS // 2
+
+    def copy(src, dst, sems, at, where):
+        return pltpu.make_async_remote_copy(
+            src_ref=src,
+            dst_ref=dst,
+            send_sem=sems[0].at[at],
+            recv_sem=sems[1].at[at],
+            device_id=where,
+            device_id_type=pl.DeviceIdType.MESH,
+        )
+
+    peers = [(b, s ^ bit) for bit in shard_bits] + [(b ^ bit, s) for bit in batch_bits]
+    barrier = pltpu.get_barrier_semaphore()
+    for peer in peers:
+        pl.semaphore_signal(
+            barrier, inc=1, device_id=peer, device_id_type=pl.DeviceIdType.MESH
+        )
+    pl.semaphore_wait(barrier, len(peers))
+
+    sems = (send_sem, recv_sem)
+    small_sems = (small_send, small_recv)
+    waits = []
+
+    def begin(op):
+        op.start()
+        waits.append(op)
+        return op
+
+    def piece(owner, c):
+        at = lax.rem(owner * per + c * per // CHUNKS + 8, NMAT)
+        if rows == D:
+            return grad_ref.at[at]
+        step = D // rows
+        return grad_ref.at[at, pl.ds((c % step) * rows, rows)]
+
+    far = shard_bits[1]
+    first = {}
+    for c in range(CHUNKS):
+        first[c] = [
+            begin(copy(piece(s ^ 1 ^ far, c), got_a.at[c, 0], sems, (c, 0), peers[0])),
+            begin(copy(piece(s ^ 1, c), got_a.at[c, 1], sems, (c, 1), peers[0])),
+        ]
+
+    small[...] = jnp.zeros_like(small)
+    stu_count, cls_count = stu_ref.shape[0], cls_ref.shape[0]
+    small[0:stu_count, :] = stu_ref[...].astype(BF16)
+    small[STU_ROWS : STU_ROWS + cls_count, 0:CLS] = cls_ref[...].astype(BF16)
+    for i in range(4):
+        at = STU_ROWS + CLS_ROWS + i * VEC_ROWS
+        lanes = slice(i * LANES, (i + 1) * LANES)
+        small[at : at + 3, :] = at_vec[0:3, lanes].astype(BF16)
+        small[at + 3 : at + NMAT, :] = ff_vec[3:NMAT, lanes].astype(BF16)
+    core = lax.rem(s, 2)
+    mine = pl.ds(pl.multiple_of(core * half, 16), half)
+    other = pl.ds(pl.multiple_of((1 - core) * half, 16), half)
+    small_op = begin(copy(small.at[other], small_got.at[0], small_sems, 0, peers[0]))
+
+    def add(x, y):
+        return (x.astype(F32) + y.astype(F32)).astype(BF16)
+
+    second = {}
+
+    def start_second(c):
+        for i, op in enumerate(first[c]):
+            op.wait_recv()
+            owner = s ^ far if i == 0 else s
+            sum_a[c, i] = add(piece(owner, c)[...], got_a[c, i])
+        second[c] = begin(copy(sum_a.at[c, 0], got_b.at[c], sems, (c, 2), peers[1]))
+
+    start_second(0)
+    start_second(1)
+
+    spans = []
+    size = rows
+    for bit in batch_bits:
+        halving = size >= 32
+        spans.append((bit, size, halving))
+        if halving:
+            size //= 2
+    offset_of = []
+    offset = jnp.int32(0)
+    slot_of = []
+    slot = 0
+    for bit, now, halving in spans:
+        place = lax.rem(b // bit, 2)
+        offset_of.append((offset, place))
+        slot_of.append(slot)
+        if halving:
+            offset = offset + place * (now // 2)
+            slot += now // 2
+        else:
+            slot += now
+    last = offset
+
+    def ranged(ref, c, start, count):
+        return ref.at[c, pl.ds(pl.multiple_of(start, 16), count)]
+
+    moving = {}
+
+    def start_batch(c, k):
+        bit, now, halving = spans[k]
+        start, place = offset_of[k]
+        if halving:
+            count = now // 2
+            src = ranged(part.at[k], c, start + (1 - place) * count, count)
+        else:
+            count = now
+            src = ranged(part.at[k], c, start, count)
+        dst = got_c.at[c, pl.ds(slot_of[k], count)]
+        moving[c, k] = begin(copy(src, dst, sems, (c, 3 + k), (b ^ bit, s)))
+
+    def end_batch(c, k):
+        bit, now, halving = spans[k]
+        start, place = offset_of[k]
+        moving[c, k].wait_recv()
+        count = now // 2 if halving else now
+        if halving:
+            start = start + place * count
+        here = pl.ds(pl.multiple_of(start, 16), count)
+        total = add(part[k, c, here, :], got_c[c, slot_of[k] : slot_of[k] + count])
+        if k + 1 < len(spans):
+            part[k + 1, c, here, :] = total
+        else:
+            final[c, here, :] = total
+
+    gathers = [k for k in reversed(range(len(spans))) if spans[k][2]]
+    gathering = {}
+
+    def start_gather(c, g):
+        k = gathers[g]
+        bit, now, _ = spans[k]
+        start, place = offset_of[k]
+        count = now // 2
+        at = ranged(final, c, start + place * count, count)
+        gathering[c, g] = begin(
+            copy(at, at, sems, (c, 3 + len(spans) + g), (b ^ bit, s))
+        )
+
+    def stage(c, k):
+        if k == 0:
+            second[c].wait_recv()
+            if c + 2 < CHUNKS:
+                start_second(c + 2)
+            part[0, c] = add(sum_a[c, 1], got_b[c])
+            start_batch(c, 0)
+        elif k <= len(spans):
+            end_batch(c, k - 1)
+            if k < len(spans):
+                start_batch(c, k)
+            else:
+                start_gather(c, 0)
+        else:
+            g = k - len(spans) - 1
+            gathering[c, g].wait_recv()
+            if g + 1 < len(gathers):
+                start_gather(c, g + 1)
+            else:
+                per_block = CHUNKS // per
+                block, within = c // per_block, c % per_block
+                own_ref[block, within * rows : (within + 1) * rows, :] = final[c]
+
+    stages = 1 + len(spans) + len(gathers)
+    rest = [(b, s ^ bit) for bit in shard_bits[1:]] + [(b ^ bit, s) for bit in batch_bits]
+
+    def small_stage(k):
+        nonlocal small_op
+        small_op.wait_recv()
+        if k == 0:
+            small_sum[0] = add(small[mine, :], small_got[0])
+        elif k <= len(rest):
+            small_sum[k] = add(small_sum[k - 1], small_got[k])
+        if k < len(rest):
+            small_op = begin(
+                copy(small_sum.at[k], small_got.at[k + 1], small_sems, k + 1, rest[k])
+            )
+        elif k == len(rest):
+            small_end[mine, :] = small_sum[k]
+            small_op = begin(
+                copy(small_sum.at[k], small_end.at[mine], small_sems, k + 1, peers[0])
+            )
+
+    small_k = 0
+    for tick in range(CHUNKS + stages - 1):
+        for k in reversed(range(stages)):
+            c = tick - k
+            if 0 <= c < CHUNKS:
+                stage(c, k)
+        if small_k <= len(rest) + 1:
+            small_stage(small_k)
+            small_k += 1
+    while small_k <= len(rest) + 1:
+        small_stage(small_k)
+        small_k += 1
+
+    for i in range(4):
+        at = STU_ROWS + CLS_ROWS + i * VEC_ROWS
+        lanes = slice(i * LANES, (i + 1) * LANES)
+        vec_out[:, lanes] = small_end[at : at + VEC_ROWS, :].astype(F32)
+    stu_out[...] = small_end[0:STU_ROWS, :].astype(F32)
+    cls_out[...] = small_end[STU_ROWS : STU_ROWS + CLS_ROWS, :].astype(F32)
+    for op in waits:
+        op.wait_send()
+
+
+def reduce_grads(grads, ff_vec, at_vec, stu, cls):
+    group, owners = lax.axis_size("batch"), lax.axis_size("shard")
+    per = NMAT // owners
+    rows = per * D // CHUNKS
+    batch_count = len(bits_of(group))
+    copies = 3 + 2 * batch_count
+    small_count = len(bits_of(owners)) + batch_count + 1
+    vmem = pl.BlockSpec(memory_space=pltpu.VMEM)
+    return pl.pallas_call(
+        functools.partial(reduce_kernel, group, owners),
+        in_specs=[vmem] * 5,
+        out_specs=[vmem] * 4,
+        out_shape=[
+            jax.ShapeDtypeStruct((per, D, D), BF16),
+            jax.ShapeDtypeStruct((VEC_ROWS, D), F32),
+            jax.ShapeDtypeStruct((STU_ROWS, SW), F32),
+            jax.ShapeDtypeStruct((CLS_ROWS, LANES), F32),
+        ],
+        scratch_shapes=[
+            pltpu.VMEM((CHUNKS, 2, rows, D), BF16),
+            pltpu.VMEM((CHUNKS, 2, rows, D), BF16),
+            pltpu.VMEM((CHUNKS, rows, D), BF16),
+            pltpu.VMEM((batch_count, CHUNKS, rows, D), BF16),
+            pltpu.VMEM((CHUNKS, rows + 16 * batch_count, D), BF16),
+            pltpu.VMEM((CHUNKS, rows, D), BF16),
+            pltpu.VMEM((SMALL_ROWS, LANES), BF16),
+            pltpu.VMEM((small_count - 1, SMALL_ROWS // 2, LANES), BF16),
+            pltpu.VMEM((small_count - 1, SMALL_ROWS // 2, LANES), BF16),
+            pltpu.VMEM((SMALL_ROWS, LANES), BF16),
+            pltpu.SemaphoreType.DMA((CHUNKS, copies)),
+            pltpu.SemaphoreType.DMA((CHUNKS, copies)),
+            pltpu.SemaphoreType.DMA((small_count,)),
+            pltpu.SemaphoreType.DMA((small_count,)),
+        ],
+        compiler_params=pltpu.CompilerParams(
+            collective_id=1, has_side_effects=True, vmem_limit_bytes=VMEM
+        ),
+        cost_estimate=pl.CostEstimate(
+            flops=NMAT * D * D * 4, bytes_accessed=NMAT * D * D * 8, transcendentals=0
+        ),
+    )(grads, ff_vec, at_vec, stu, cls)
+
+
+def update_kernel(
+    own_ref,
+    blocks_ref,
+    left_ref,
+    right_ref,
+    lroot_ref,
+    rroot_ref,
+    shard_ref,
+    vsum_ref,
+    vec_ref,
+    vmom_ref,
+    ssum_ref,
+    stu_ref,
+    smom_ref,
+    csum_ref,
+    cls_ref,
+    cmom_ref,
+    grad_out,
+    new_out,
+    left_out,
+    right_out,
+    vg_out,
+    vm_out,
+    v_out,
+    sg_out,
+    sm_out,
+    s_out,
+    cg_out,
+    cm_out,
+    c_out,
+    *,
+    owners,
+):
+    g = own_ref[0]
+    grad_out[0] = g.astype(F32)
+    left_out[0] = decay_rate * left_ref[0] + (1.0 - decay_rate) * nt(g, g)
+    right_out[0] = decay_rate * right_ref[0] + (1.0 - decay_rate) * tn(g, g)
+    steered = nn(lroot_ref[0].astype(BF16), g).astype(BF16)
+    steered = nn(steered, rroot_ref[0].astype(BF16))
+    size = jnp.mean(steered * steered, keepdims=True)
+    new_out[0] = blocks_ref[0].astype(F32) - steered * (block_rate * lax.rsqrt(size + 1e-06))
+
+    @pl.when(pl.program_id(0) == 0)
+    def _():
+        per = NMAT // owners
+        mine = vsum_ref[0:per, :]
+        for i in range(1, owners):
+            mine = jnp.where(shard_ref[0] == i, vsum_ref[i * per : (i + 1) * per, :], mine)
+
+        def rule(grads, old, moment, rate, outs):
+            renewed = decay_rate * moment + (1.0 - decay_rate) * grads * grads
+            outs[0][...] = grads
+            outs[1][...] = renewed
+            outs[2][...] = old - rate * grads / (jnp.sqrt(renewed) + 1e-08)
+
+        rule(mine, vec_ref[...], vmom_ref[...], vector_rate, (vg_out, vm_out, v_out))
+        rule(
+            ssum_ref[0 : stu_ref.shape[0], :],
+            stu_ref[...],
+            smom_ref[...],
+            head_rate,
+            (sg_out, sm_out, s_out),
+        )
+        rule(
+            csum_ref[0 : cls_ref.shape[0], 0:CLS],
+            cls_ref[...],
+            cmom_ref[...],
+            head_rate,
+            (cg_out, cm_out, c_out),
+        )
+
+
+def update(own, blocks, left, right, lroot, rroot, shard, vsum, vec, vmom, ssum, stu, smom, csum, cls, cmom):
+    per = own.shape[0]
+    mat = pl.BlockSpec((1, D, D), lambda i: (i, 0, 0))
+    whole = lambda a: pl.BlockSpec(a.shape, lambda i: (0,) * a.ndim)
+    like = lambda a: jax.ShapeDtypeStruct(a.shape, F32)
+    return pl.pallas_call(
+        functools.partial(update_kernel, owners=NMAT // per),
+        grid=(per,),
+        in_specs=[mat] * 6
+        + [pl.BlockSpec(memory_space=pltpu.SMEM)]
+        + [whole(a) for a in (vsum, vec, vmom, ssum, stu, smom, csum, cls, cmom)],
+        out_specs=[mat] * 4 + [whole(a) for a in (vec,) * 3 + (stu,) * 3 + (cls,) * 3],
+        out_shape=[like(left)] * 4 + [like(a) for a in (vec,) * 3 + (stu,) * 3 + (cls,) * 3],
+        compiler_params=pltpu.CompilerParams(vmem_limit_bytes=VMEM),
+    )(own, blocks, left, right, lroot, rroot, shard, vsum, vec, vmom, ssum, stu, smom, csum, cls, cmom)
 
 
 def local(
@@ -795,56 +1170,31 @@
         info, a1, matrices, vec, student, classifier, goals, send, send.reshape(-1, 1), returned
     )
     arrived = lax.all_to_all(outgoing, "batch", split_axis=0, concat_axis=0, tiled=True)
-    input_grads, at_grads, at_vecs = attend_back(
-        info, tokens, da1.reshape(micro, row_len, D), q, k, v, o, matrices
+    input_grads, grads, at_vecs = attend_back(
+        info, tokens, da1.reshape(micro, row_len, D), q, k, v, o, matrices, ff_grads
     )
     layer_out = place_rows(back[:, None, :], arrived)
-
-    grads = jnp.concatenate([at_grads, ff_grads], axis=0)
-    vec_grads = jnp.concatenate([at_vecs[:3], ff_vecs[3:]], axis=0)
-    owned = lax.psum_scatter(grads, "shard", scatter_dimension=0, tiled=True)
-    owned = lax.psum(owned, "batch")
-    small = jnp.concatenate(
-        [vec_grads.reshape(-1), stu_grads.reshape(-1), cls_grads.reshape(-1)]
+    own, vec_sum, stu_sum, cls_sum = reduce_grads(grads, ff_vecs, at_vecs, stu_grads, cls_grads)
+    shard = lax.axis_index("shard").astype(jnp.int32).reshape(1)
+    updated = update(
+        own,
+        blocks,
+        left_stats,
+        right_stats,
+        left_root,
+        right_root,
+        shard,
+        vec_sum,
+        vectors,
+        vec_moment,
+        stu_sum,
+        student,
+        stu_moment,
+        cls_sum,
+        classifier,
+        cls_moment,
     )
-    small = lax.psum(small, ("batch", "shard"))
-    whole_vecs = small[: NMAT * D].reshape(NMAT, D)
-    head_student = small[NMAT * D : NMAT * D + student.size].reshape(student.shape)
-    head_class = small[NMAT * D + student.size :].reshape(classifier.shape)
-    owners = lax.axis_size("shard")
-    owned_vecs = lax.dynamic_slice_in_dim(
-        whole_vecs, lax.axis_index("shard") * (NMAT // owners), NMAT // owners, 0
-    )
-
-    owned_f32 = owned.astype(F32)
-    gram_left = jnp.einsum("bij,bkj->bik", owned, owned, preferred_element_type=F32)
-    gram_right = jnp.einsum("bji,bjk->bik", owned, owned, preferred_element_type=F32)
-    new_left = decay_rate * left_stats + (1.0 - decay_rate) * gram_left
-    new_right = decay_rate * right_stats + (1.0 - decay_rate) * gram_right
-    steered = jnp.einsum("bij,bjk->bik", left_root, owned_f32)
-    steered = jnp.einsum("bij,bjk->bik", steered, right_root)
-    size_norm = jnp.sqrt(jnp.mean(steered * steered, axis=(1, 2), keepdims=True) + 1e-06)
-    new_blocks = blocks.astype(F32) - block_rate * steered / size_norm
-    new_vec_moment, new_vectors = diagonal_rule(vectors, vec_moment, owned_vecs, vector_rate)
-    new_stu_moment, new_student = diagonal_rule(student, stu_moment, head_student, head_rate)
-    new_cls_moment, new_classifier = diagonal_rule(classifier, cls_moment, head_class, head_rate)
-    return (
-        layer_out[:, None],
-        input_grads[:, None],
-        owned_f32,
-        new_blocks,
-        new_left,
-        new_right,
-        owned_vecs,
-        new_vec_moment,
-        new_vectors,
-        head_student,
-        new_stu_moment,
-        new_student,
-        head_class,
-        new_cls_moment,
-        new_classifier,
-    )
+    return (layer_out[:, None], input_grads[:, None], *updated)
 
 
 def solution(mesh):

time: 576 us -> 375 us (0.65)
  waiting for transfers between devices: 271 us -> 7.86 us
  Pallas kernels: 173 us -> 300 us
  starting transfers between devices: 44.5 us -> 10.6 us
  other arithmetic: 31.4 us -> 9.02 us
  matrix products: 11.2 us -> 0 us
    psum x2 -> x0, waiting for transfers between devices: 214 us -> none  [the longest x1 133 us: local(): small = lax.psum(small, ('batch', 'shard'))]
    pallas_call x0 -> x2, Pallas kernels: none -> 111 us  [the longest x1 95.8 us: reduce_grads(): pl.pallas_call(functools.partial(reduce_kernel, group, owners), in_specs=...]
    reduce_scatter x1 -> x0, waiting for transfers between devices: 56.2 us -> none  [local(): owned = lax.psum_scatter(grads, 'shard', scatter_dimension=0, tiled=True)]
    all_to_all x1, starting transfers between devices: 39.9 us -> 6.02 us  [local(): lax.all_to_all(outgoing, 'batch', split_axis=0, concat_axis=0, tiled=True)]
    dot_general x3 -> x0, matrix products: 11.2 us -> none  [the longest x1 5.83 us: local(): steered = jnp.einsum('bij,bjk->bik', steered, right_root)]
    sub x4 -> x0, other arithmetic: 9.66 us -> none  [the longest x3 4.91 us: diagonal_rule(): old_values - rate * grads / (jnp.sqrt(new_moment) + 1e-08)]
    pallas_call x1, Pallas kernels: 32.8 us -> 41.1 us  [attend(): pl.pallas_call(attend_kernel, grid=(micro,), in_specs=[pl.BlockSpec(memor...]
    pallas_call x1, Pallas kernels: 44.5 us -> 52.8 us  [attend_back(): pl.pallas_call(functools.partial(attend_back_kernel, micro=micro), grid=(...]
  transfers between devices with their start and end apart: 6 -> 3, of which waited for: 3 -> 1; matrix products, arithmetic and copies ran while one was open for 6% -> 6% of each run, Pallas kernels for 7% -> 56%
where the time goes in v2:
time: 375 us
  Pallas kernels  300 us (80%)
  blocking collectives  18.6 us (5%)
  between operations  15.1 us (4%)
  local copies, waits for them, and re-layouts  13.2 us (4%)
  starting transfers between devices  10.6 us (3%)
  other arithmetic  9.02 us (2%)
  waiting for transfers between devices  7.86 us (2%)
    pallas_call x1, Pallas kernels, reduce_grads(): pl.pallas_call(functools.partial(reduce_kernel, group, owners), in_specs=...  95.8 us
    pallas_call x1, Pallas kernels, feed(): pl.pallas_call(functools.partial(feed_kernel, tile=tile, micro=micro, row...  86.2 us
    pallas_call x1, Pallas kernels, attend_back(): pl.pallas_call(functools.partial(attend_back_kernel, micro=micro), grid=(...  52.8 us
    pallas_call x1, Pallas kernels, attend(): pl.pallas_call(attend_kernel, grid=(micro,), in_specs=[pl.BlockSpec(memor...  41.1 us
    pallas_call x1, Pallas kernels, update(): pl.pallas_call(functools.partial(update_kernel, owners=NMAT // per), grid...  14.9 us
    unnamed x1, blocking collectives  13.1 us
    unnamed x26, local copies, waits for them, and re-layouts  10.3 us
  transfers between devices with their start and end apart: 3, of which 1 were waited for; matrix products, arithmetic and copies ran while one was open for 6% of the time, Pallas kernels for 56%

profile of v2, /device:TPU:0, one launch (start us, length us, event | category | flops | bytes accessed | tf_op | source)
XLA Modules:
  0.0 374.7 jit_solution(17207525612647141223)
XLA Ops:
  7.2 0.7 all-gather.4.cloned.1.call-update
  7.9 1.2 dynamic-slice
  9.8 0.7 broadcast_select_fusion
  10.5 0.8 fusion.25
  11.6 13.1 %all-reduce = s32[16]{0:T(128)S(1)} all-reduce(s32[16]{0:T(128)S(1)} %dynamic-update-slice), channel_id=2, replica_groups=mesh['batch'=8,'shard'=4] {'batch'}, use_global_device_ids=true, to_apply=%add | all-reduce | flops 16 | bytes 128
  25.0 0.9 reshape.505
  25.9 0.9 reshape.506
  26.8 2.1 fusion.8.place_ref
  28.9 5.0 %shard_map.272 = bf16[8,2,128,512]{3,2,1,0:T(8,128)(2,1)} custom-call(s32[2,1024,1]{2,1,0:T(8,128)} %fusion.8.place_ref, bf16[2,1024,512]{2,1,0:T(8,128)(2,1)} %bitcast.79), custom_call_target="tpu_custom_call" | custom-call | tf_op jit(solution)/shard_map/pallas_call | solution.py:701
  33.9 4.5 %all-to-all-start = ((bf16[8,2,128,512]{3,2,1,0:T(8,128)(2,1)}), bf16[8,2,128,512]{3,2,1,0:T(8,128)(2,1)}, u32[]{:S(2)}, u32[]{:S(2)}) async-start(bf16[8,2,128,512]{3,2,1,0:T(8,128)(2,1)} %shard_map.272), calls=%async_computation | async-start | bytes 4194304 | tf_op jit(solution)/shard_map/all_to_all | solution.py:1160
  38.6 5.6 %all-gather.1 = bf16[4,3,512]{2,1,0:T(4,128)(2,1)S(1)} all-gather(bf16[1,3,512]{2,1,0:T(4,128)(2,1)S(1)} %convert_bitcast_fusion), channel_id=1, replica_groups=mesh['batch'=8,'shard'=4] {'shard'}, dimensions={0}, use_global_device_ids=true | all-gather | bytes 15360 | tf_op jit(solution)/shard_map/all_gather | solution.py:1163
  44.2 0.6 reshape.502.vec_ref
  44.9 0.7 copy.111.cls_ref
  46.2 0.7 fusion.20
  47.3 0.5 copy.120
  48.2 0.6 pad_add_fusion.info
  48.8 0.7 pad_maximum_fusion.goal_ref
  49.5 2.1 fusion.3.send_col
  51.6 7.2 %all-gather.4.cloned.1.call-done.w_ref = bf16[12,512,512]{2,1,0:T(8,128)(2,1)} async-done(((bf16[3,512,512]{2,1,0:T(8,128)(2,1)}), bf16[12,512,512]{2,1,0:T(8,128)(2,1)}) %all-gather.4.cloned.1.call-update) | async-done | bytes 6291472 | tf_op jit(solution)/shard_map/all_gather | solution.py:1162
  58.8 41.1 %shard_map.271 = (f32[2,1024,512]{2,1,0:T(8,128)}, bf16[2,1024,1024]{2,1,0:T(8,128)(2,1)}, bf16[2,1024,512]{2,1,0:T(8,128)(2,1)}, bf16[2,1024,512]{2,1,0:T(8,128)(2,1)}, bf16[2,1024,512]{2,1,0:T(8,128)(2,1)}) custom-call(s32[2,8]{1,0:T(2,128)} %pad_add_fusion.info, bf16[2,1024,512]{2,1,0:T(8,128)(2,1)} %bitcast.95, ...), custom_call_target="tpu_custom_call" | custom-call | flops 8589934592 | bytes 16777216 | tf_op jit(solution)/shard_map/pallas_call | solution.py:204
  99.8 86.2 %shard_map.273 = (f32[2048,512]{1,0:T(8,128)}, bf16[8,2,128,512]{3,2,1,0:T(8,128)(2,1)}, bf16[12,512,512]{2,1,0:T(8,128)(2,1)}, f32[12,512]{1,0:T(8,128)}, f32[643,128]{1,0:T(8,128)}, /*index=5*/f32[129,14]{1,0:T(8,128)}) custom-call(s32[2,8]{1,0:T(2,128)} %pad_add_fusion.info, f32[2048,512]{1,0:T(8,128)} %bitcast.98, ...), custom_call_target="tpu_custom_call" | custom-call | flops 25769803776 | bytes 16777216 | tf_op jit(solution)/shard_map/pallas_call | solution.py:454
  186.1 6.0 %all-to-all-start.1 = ((bf16[8,2,128,512]{3,2,1,0:T(8,128)(2,1)}), bf16[8,2,128,512]{3,2,1,0:T(8,128)(2,1)S(1)}, u32[]{:S(2)}, u32[]{:S(2)}) async-start(bf16[8,2,128,512]{3,2,1,0:T(8,128)(2,1)} %get-tuple-element.47), calls=%async_computation.1 | async-start | bytes 4194304 | tf_op jit(solution)/shard_map/all_to_all | solution.py:1172
  192.1 0.7 copy.113.cmom_ref
  192.8 0.7 compare_select_fusion.2.place_ref
  193.5 52.8 %shard_map.275 = (bf16[2,1024,512]{2,1,0:T(8,128)(2,1)}, bf16[12,512,512]{2,1,0:T(8,128)(2,1)}, f32[8,512]{1,0:T(8,128)}) custom-call(s32[2,8]{1,0:T(2,128)} %pad_add_fusion.info, bf16[2,1024,512]{2,1,0:T(8,128)(2,1)} %bitcast.96, f32[2,1024,512]{2,1,0:T(8,128)} %bitcast.97, ...), custom_call_target="tpu_custom_call", output_to_operand_aliasing={{1}: (8, {})} | custom-call | flops 19327352832 | bytes 16777216 | tf_op jit(solution)/shard_map/pallas_call | solution.py:647
  246.3 95.8 %shard_map.276 = (bf16[3,512,512]{2,1,0:T(8,128)(2,1)}, f32[16,512]{1,0:T(8,128)}, f32[656,128]{1,0:T(8,128)}, f32[144,128]{1,0:T(8,128)}) custom-call(bf16[12,512,512]{2,1,0:T(8,128)(2,1)} %get-tuple-element.55.grad_ref, f32[12,512]{1,0:T(8,128)} %get-tuple-element.56.ff_vec, f32[8,512]{1,0:T(8,128)} %get-tuple-element.57.at_vec, ...), custom_call_target="tpu_custom_call" | custom-call | flops 12582912 | bytes 25165824 | tf_op jit(solution)/shard_map/pallas_call | solution.py:990
  342.0 14.9 %shard_map.277 = (f32[3,512,512]{2,1,0:T(8,128)}, f32[3,512,512]{2,1,0:T(8,128)}, f32[3,512,512]{2,1,0:T(8,128)}, f32[3,512,512]{2,1,0:T(8,128)}, f32[3,512]{1,0...) custom-call(bf16[3,512,512]{2,1,0:T(8,128)(2,1)} %get-tuple-element., ...), custom_call_target="tpu_custom_call" | custom-call | tf_op jit(solution)/shard_map/pallas_call | solution.py:1102
  356.9 1.6 copy.116
  358.5 1.6 copy.117
  360.1 1.6 copy.118
  361.6 1.4 copy-done
  363.0 4.7 %shard_map.274 = bf16[2,1024,512]{2,1,0:T(8,128)(2,1)} custom-call(s32[2,1,1024]{2,1,0:T(1,128)} %compare_select_fusion.2.place_ref, bf16[8,2,128,512]{3,2,1,0:T(8,128)(2,1)} %copy-done), custom_call_target="tpu_custom_call" | custom-call | tf_op jit(solution)/shard_map/pallas_call | solution.py:724
  (40 shorter events, 2.3 us)
Async XLA Ops:
  7.2 51.6 %all-gather.4.cloned.1.call-start = ((), (), s32[]{:S(2)}) async-start(), calls=%async_computation.2 | async-start | bytes 7864320 | tf_op jit(solution)/shard_map/all_gather | solution.py:1162
  33.9 4.5 %copy-start.2 = (s32[2,1,4]{2,1,0:T(1,128)S(1)}, s32[2,1,4]{2,1,0:T(1,128)}, u32[]{:S(2)}) copy-start(s32[2,1,4]{2,1,0:T(1,128)} %param.18) | copy-start | bytes 100
  33.9 4.7 %copy-start.1 = (f32[3,512]{1,0:T(4,128)S(1)}, f32[3,512]{1,0:T(4,128)}, u32[]{:S(2)}) copy-start(f32[3,512]{1,0:T(4,128)} %vec_ref.1) | copy-start | bytes 18436
  33.9 11.0 %copy-start.3 = (f32[129,14]{0,1:T(8,128)S(1)}, f32[129,14]{0,1:T(8,128)}, u32[]{:S(2)}) copy-start(f32[129,14]{0,1:T(8,128)} %param.30) | copy-start | bytes 21676
  33.9 14.9 %copy-start.5 = (f32[2,1,4,14]{3,2,1,0:T(4,128)S(1)}, f32[2,1,4,14]{3,2,1,0:T(4,128)}, u32[]{:S(2)}) copy-start(f32[2,1,4,14]{3,2,1,0:T(4,128)} %param.20) | copy-start | bytes 1348
  33.9 65.9 %all-to-all-start = ((bf16[8,2,128,512]{3,2,1,0:T(8,128)(2,1)}), bf16[8,2,128,512]{3,2,1,0:T(8,128)(2,1)}, u32[]{:S(2)}, u32[]{:S(2)}) async-start(bf16[8,2,128,512]{3,2,1,0:T(8,128)(2,1)} %shard_map.272), calls=%async_computation | async-start | bytes 4194304 | tf_op jit(solution)/shard_map/all_to_all | solution.py:1160
  186.1 6.0 %copy-start.4 = (f32[129,14]{0,1:T(8,128)S(1)}, f32[129,14]{0,1:T(8,128)}, u32[]{:S(2)}) copy-start(f32[129,14]{0,1:T(8,128)} %param.31) | copy-start | bytes 21676
  186.1 175.6 %all-to-all-start.1 = ((bf16[8,2,128,512]{3,2,1,0:T(8,128)(2,1)}), bf16[8,2,128,512]{3,2,1,0:T(8,128)(2,1)S(1)}, u32[]{:S(2)}, u32[]{:S(2)}) async-start(bf16[8,2,128,512]{3,2,1,0:T(8,128)(2,1)} %get-tuple-element.47), calls=%async_computation.1 | async-start | bytes 4194304 | tf_op jit(solution)/shard_map/all_to_all | solution.py:1172
  361.6 1.4 copy-start
Sparse Core Ops, SparseCore 0:
  9.6 49.1 all-gather.3

commit v3 on v2

--- a/solution.py
+++ b/solution.py
@@ -26,6 +26,8 @@
 KG = 128
 PAIRS = H // 2
 LANES = 128
+PART = 512
+PARTS, CUT = FF // PART, D // PART
 BIG = float(2**30)
 EPS = 1e-6
 VMEM = 60 * 1024 * 1024
@@ -54,6 +56,11 @@
 
 def row_sum(v):
     return jnp.sum(v, axis=0, keepdims=True)
+
+
+def two_low(v, b):
+    high = v.astype(BF16)
+    return nn(high, b) + nn((v - high.astype(F32)).astype(BF16), b)
 
 
 def split_low(v):
@@ -97,134 +104,133 @@
     return lax.broadcasted_iota(jnp.int32, (rows, LANES), 1)
 
 
-def key_spare(sample, rows):
+TAG = 16
+
+
+def key_spare(sample, rows, pair):
     lane = lane_index(rows) % DH
-    return jnp.where(
-        lane < SAMP, (lane == sample).astype(F32), (lane < SAMP + 3).astype(F32)
-    )
+    own = (lane < 3 * PAIRS) & (lane % PAIRS == pair)
+    return jnp.where(own | (lane == sample + TAG), 1.0, 0.0)
 
 
 def query_spare(sample, rows):
     lane = lane_index(rows) % DH
-    return jnp.where((lane < SAMP) & (lane != sample), -BIG, 0.0)
-
-
-def halves(pair, spare, first):
-    return jnp.where(first, pair, spare), jnp.where(first, spare, pair)
-
-
-def attend_kernel(
-    info, x_ref, w_ref, vec_ref, a1_ref, q_ref, k_ref, v_ref, o_ref, kx, vx
-):
+    tag = (lane >= TAG) & (lane < TAG + SAMP) & (lane != sample + TAG)
+    return jnp.where(tag, -BIG, 0.0)
+
+
+def store_heads(ref, rows, p, pair, spare, first):
+    ref[rows, 2 * p * LANES : (2 * p + 1) * LANES] = jnp.where(first, pair, spare).astype(BF16)
+    ref[rows, (2 * p + 1) * LANES : (2 * p + 2) * LANES] = jnp.where(
+        first, spare, pair
+    ).astype(BF16)
+
+
+def head_lanes(h):
+    return slice(h * LANES, (h + 1) * LANES)
+
+
+def widths(row_len):
+    most = row_len // KG
+    return list(range(most // 2, most + 1))
+
+
+def chosen_span(ends, live, t, row_len):
+    begin, number = reach(ends, live, t * QT, QT, row_len)
+    least, most = widths(row_len)[0], row_len // KG
+    number = jnp.where(number > 0, jnp.maximum(number, least), 0)
+    return jnp.minimum(begin, most - number), number
+
+
+def attend_kernel(info, x_ref, w_ref, vec_ref, q_ref, k_ref, v_ref, o_ref, l_ref, qx, kx, vx):
     row = pl.program_id(0)
     row_len = x_ref.shape[1]
     ends, live = ends_of(info, row), live_of(info, row)
     first = lane_index(QT) < DH
+    ones = jnp.ones((QT, LANES), F32)
 
     @pl.loop(0, row_len // QT)
     def _(t):
         rows = pl.ds(pl.multiple_of(t * QT, QT), QT)
         x = x_ref[0, rows, :]
         sample = sample_column(ends, t * QT, QT)
-        k_extra, q_extra = key_spare(sample, QT), query_spare(sample, QT)
-        q = (nn(x, w_ref[0]) + vec_ref[0:1, :]).astype(BF16).astype(F32) * DH**-0.5
+        q_extra = query_spare(sample, QT)
+        q = ((nn(x, w_ref[0]) + vec_ref[0:1, :]).astype(BF16).astype(F32) * DH**-0.5).astype(BF16)
         k = nn(x, w_ref[1]).astype(BF16)
         v = (nn(x, w_ref[2]) + vec_ref[1:2, :]).astype(BF16)
+        q_ref[0, rows, :] = q
         k_ref[0, rows, :] = k
         v_ref[0, rows, :] = v
         for p in range(PAIRS):
-            pair = slice(p * LANES, (p + 1) * LANES)
-            for ref, values, spare in (
-                (q_ref.at[0], q, q_extra),
-                (kx, k.astype(F32), k_extra),
-                (vx, v.astype(F32), jnp.ones((QT, LANES), F32)),
-            ):
-                left, right = halves(values[:, pair], spare, first)
-                ref[rows, 2 * p * LANES : (2 * p + 1) * LANES] = left.astype(BF16)
-                ref[rows, (2 * p + 1) * LANES : (2 * p + 2) * LANES] = right.astype(BF16)
+            pair = head_lanes(p)
+            store_heads(qx, rows, p, q[:, pair].astype(F32), q_extra, first)
+            store_heads(kx, rows, p, k[:, pair].astype(F32), key_spare(sample, QT, p), first)
+            store_heads(vx, rows, p, v[:, pair].astype(F32), ones, first)
 
     @pl.loop(0, row_len // QT)
     def _(t):
         rows = pl.ds(pl.multiple_of(t * QT, QT), QT)
-        begin, number = reach(ends, live, t * QT, QT, row_len)
+        begin, number = chosen_span(ends, live, t, row_len)
 
         @pl.when(number == 0)
         def _():
             o_ref[0, rows, :] = jnp.zeros((QT, D), BF16)
-
-        for n in range(1, row_len // KG + 1):
+            l_ref[0, rows, :] = jnp.zeros((QT, LANES), F32)
+
+        for n in widths(row_len):
 
             @pl.when(number == n)
             def _(n=n):
                 span = pl.ds(pl.multiple_of(begin * KG, KG), n * KG)
                 lane = lane_index(QT)
-
-                @pl.loop(0, PAIRS)
-                def _(p):
-                    parts = []
-                    for head in range(2):
-                        cols = pl.ds(
-                            pl.multiple_of((2 * p + head) * LANES, LANES), LANES
-                        )
-                        q = q_ref[0, rows, cols]
-                        s = nt(q, kx[span, cols])
+                scores, powers, got = {}, {}, {}
+                peaks = jnp.zeros((QT, LANES), F32)
+                totals = jnp.ones((QT, LANES), F32)
+                for step in range(H + 2):
+                    if step < H:
+                        cols = head_lanes(step)
+                        scores[step] = nt(qx[rows, cols], kx[span, cols])
+                    h = step - 1
+                    if 0 <= h < H:
+                        s = scores.pop(h)
                         peak = jnp.max(s, axis=1, keepdims=True)
-                        e = jnp.exp(s - peak).astype(BF16)
-                        got = nn(e, vx[span, cols])
-                        parts.append(got)
-                        other = (lane >= DH) if head == 0 else (lane < DH)
-                        total = peak + jnp.log(jnp.where(other, got, 1.0))
-                        high, mid, rest = split_low(
-                            jnp.where(peak > -0.5 * BIG, total, 0.0)
-                        )
-                        at = lane % DH
-                        fill = jnp.where(
-                            at == SAMP, -high, jnp.where(at == SAMP + 1, -mid, -rest)
-                        )
-                        spot = other & (at >= SAMP) & (at < SAMP + 3)
-                        q_ref[0, rows, cols] = jnp.where(
-                            spot, fill, q.astype(F32)
-                        ).astype(BF16)
-                    top = jnp.where(first, parts[0], parts[1])
-                    total = pltpu.roll(jnp.where(first, parts[1], parts[0]), DH, 1)
-                    cols = pl.ds(pl.multiple_of(p * LANES, LANES), LANES)
-                    o_ref[0, rows, cols] = (top / total).astype(BF16)
-
-    @pl.loop(0, row_len // QT)
-    def _(t):
-        rows = pl.ds(pl.multiple_of(t * QT, QT), QT)
-        a1_ref[0, rows, :] = x_ref[0, rows, :].astype(F32) + (
-            nn(o_ref[0, rows, :], w_ref[3]) + vec_ref[2:3, :]
-        )
+                        powers[h] = jnp.exp(s - peak).astype(BF16)
+                        spot = lane == (h // 2 + DH if h % 2 == 0 else h // 2)
+                        peaks = jnp.where(spot, peak, peaks)
+                    h = step - 2
+                    if 0 <= h < H:
+                        got[h] = nn(powers.pop(h), vx[span, head_lanes(h)])
+                        spot = lane == (h // 2 + DH if h % 2 == 0 else h // 2)
+                        totals = jnp.where(spot, got[h], totals)
+                        if h % 2 == 1:
+                            left, right = got.pop(h - 1), got.pop(h)
+                            top = jnp.where(first, left, right)
+                            total = pltpu.roll(jnp.where(first, right, left), DH, 1)
+                            o_ref[0, rows, head_lanes(h // 2)] = (top / total).astype(BF16)
+                l_ref[0, rows, :] = jnp.where(
+                    peaks > -0.5 * BIG, peaks + jnp.log(totals), 0.0
+                )
 
 
 def attend(info, tokens, blocks, vec):
     micro, row_len, _ = tokens.shape
     row_spec = lambda width: pl.BlockSpec((1, row_len, width), lambda r: (r, 0, 0))
+    low = jax.ShapeDtypeStruct((micro, row_len, D), BF16)
     return pl.pallas_call(
         attend_kernel,
         grid=(micro,),
         in_specs=[
             pl.BlockSpec(memory_space=pltpu.SMEM),
             row_spec(D),
-            pl.BlockSpec((4, D, D), lambda r: (0, 0, 0)),
+            pl.BlockSpec((3, D, D), lambda r: (0, 0, 0)),
             pl.BlockSpec((NMAT, D), lambda r: (0, 0)),
         ],
-        out_specs=[row_spec(D), row_spec(2 * D), row_spec(D), row_spec(D), row_spec(D)],
-        out_shape=[
-            jax.ShapeDtypeStruct((micro, row_len, D), F32),
-            jax.ShapeDtypeStruct((micro, row_len, 2 * D), BF16),
-            jax.ShapeDtypeStruct((micro, row_len, D), BF16),
-            jax.ShapeDtypeStruct((micro, row_len, D), BF16),
-            jax.ShapeDtypeStruct((micro, row_len, D), BF16),
-        ],
-        scratch_shapes=[
-            pltpu.VMEM((row_len, 2 * D), BF16),
-            pltpu.VMEM((row_len, 2 * D), BF16),
-        ],
+        out_specs=[row_spec(D)] * 4 + [row_spec(LANES)],
+        out_shape=[low] * 4 + [jax.ShapeDtypeStruct((micro, row_len, LANES), F32)],
+        scratch_shapes=[pltpu.VMEM((row_len, 2 * D), BF16)] * 3,
         compiler_params=pltpu.CompilerParams(vmem_limit_bytes=VMEM),
         cost_estimate=pl.CostEstimate(
-            flops=micro * row_len * D * D * 8 + micro * H * row_len * row_len * DH * 4,
+            flops=micro * row_len * D * D * 6 + micro * H * row_len * row_len * DH * 16,
             bytes_accessed=micro * row_len * D * 16,
             transcendentals=micro * H * row_len * row_len,
         ),
@@ -232,18 +238,9 @@
 
 
 def gelu_both(u):
-    t = 1.0 / (1.0 + (0.3275911 * 0.5**0.5) * jnp.abs(u))
-    bell = jnp.exp(-0.5 * (u * u))
-    tail = (
-        t
-        * (
-            0.127414796
-            + t * (-0.142248368 + t * (0.7107068705 + t * (-0.7265760135 + t * 0.5307027145)))
-        )
-        * bell
-    )
-    share = jnp.where(u >= 0, 1.0 - tail, tail)
-    return u * share, share + u * bell * 0.3989422804014327
+    share = 0.5 + 0.5 * lax.erf(u * 0.5**0.5)
+    bell = jnp.exp2((-0.5 * 1.4426950408889634) * (u * u))
+    return u * share, share + (u * 0.3989422804014327) * bell
 
 
 def norm_parts(a):
@@ -262,7 +259,8 @@
 
 def feed_kernel(
     info,
-    a1_ref,
+    x_ref,
+    o_ref,
     w_ref,
     vec_ref,
     stu_ref,
@@ -287,7 +285,6 @@
     zb,
     head_in,
     head_low,
-    feed_low,
     *,
     tile,
     micro,
@@ -304,20 +301,29 @@
     @pl.when(step < tiles)
     def _():
         rows = pl.ds(pl.multiple_of(step * tile, tile), tile)
-        unit, rate = norm_parts(a1_ref[...])
+        a1 = x_ref[...].astype(F32) + (nn(o_ref[...], w_ref[3]) + vec_ref[2:3, :])
+        unit, rate = norm_parts(a1)
         unit1[rows, :] = unit
         rate1[rows, :] = rate
         h1 = unit * vec_ref[3:4, :] + vec_ref[4:5, :]
         low = h1.astype(BF16)
         h1b[rows, :] = low
         total = h1 + vec_ref[9:10, :]
-        for c in range(FF // D):
-            cols = slice(c * D, (c + 1) * D)
-            value, grad = gelu_both(nn(low, w_ref[4 + c]) + vec_ref[5 + c : 6 + c, :])
-            value = value.astype(BF16)
-            act[rows, cols] = value
-            slope[rows, cols] = grad.astype(BF16)
-            total = total + nn(value, w_ref[8 + c])
+        raw, value = {}, {}
+        for turn in range(PARTS + 2):
+            if turn < PARTS:
+                c, at = turn // CUT, slice(turn % CUT * PART, (turn % CUT + 1) * PART)
+                raw[turn] = nn(low, w_ref[4 + c, :, at]) + vec_ref[5 + c : 6 + c, at]
+            if 0 <= turn - 1 < PARTS:
+                cols = slice((turn - 1) * PART, turn * PART)
+                up, grad = gelu_both(raw.pop(turn - 1))
+                value[turn - 1] = up.astype(BF16)
+                act[rows, cols] = value[turn - 1]
+                slope[rows, cols] = grad.astype(BF16)
+            if 0 <= turn - 2 < PARTS:
+                c = (turn - 2) // CUT
+                at = slice((turn - 2) % CUT * PART, ((turn - 2) % CUT + 1) * PART)
+                total = total + nn(value.pop(turn - 2), w_ref[8 + c, at, :])
         unit, rate = norm_parts(total)
         unit2[rows, :] = unit
         rate2[rows, :] = rate
@@ -352,15 +358,26 @@
         vg_ref[11:12, :] += row_sum(dz)
         da2 = norm_back(dz * vec_ref[10:11, :], unit, rate2[rows, :])
         low = da2.astype(BF16)
-        feed_low[rows, :] = low
+        zb[rows, :] = low
         vg_ref[9:10, :] += row_sum(low.astype(F32))
         dh1 = da2
-        for c in range(FF // D):
-            cols = slice(c * D, (c + 1) * D)
-            du = (nt(low, w_ref[8 + c]) * slope[rows, cols].astype(F32)).astype(BF16)
-            slope[rows, cols] = du
-            vg_ref[5 + c : 6 + c, :] += row_sum(du.astype(F32))
-            dh1 = dh1 + nt(du, w_ref[4 + c])
+        raw, value = {}, {}
+        for turn in range(PARTS + 2):
+            if turn < PARTS:
+                c, at = turn // CUT, slice(turn % CUT * PART, (turn % CUT + 1) * PART)
+                raw[turn] = nt(low, w_ref[8 + c, at, :])
+            if 0 <= turn - 1 < PARTS:
+                cols = slice((turn - 1) * PART, turn * PART)
+                c = (turn - 1) // CUT
+                at = slice((turn - 1) % CUT * PART, ((turn - 1) % CUT + 1) * PART)
+                du = (raw.pop(turn - 1) * slope[rows, cols].astype(F32)).astype(BF16)
+                value[turn - 1] = du
+                slope[rows, cols] = du
+                vg_ref[5 + c : 6 + c, at] += row_sum(du.astype(F32))
+            if 0 <= turn - 2 < PARTS:
+                c = (turn - 2) // CUT
+                at = slice((turn - 2) % CUT * PART, ((turn - 2) % CUT + 1) * PART)
+                dh1 = dh1 + nt(value.pop(turn - 2), w_ref[4 + c, :, at])
         unit = unit1[rows, :]
         vg_ref[3:4, :] += row_sum(dh1 * unit)
         vg_ref[4:5, :] += row_sum(dh1)
@@ -371,7 +388,7 @@
         for c in range(FF // D):
             cols = slice(c * D, (c + 1) * D)
             wg_ref[c] = tn(h1b[...], slope[:, cols]).astype(BF16)
-            wg_ref[4 + c] = tn(act[:, cols], feed_low[...]).astype(BF16)
+            wg_ref[4 + c] = tn(act[:, cols], zb[...]).astype(BF16)
 
 
 def head_phase(info, stu_ref, cls_ref, goal_ref, sg_ref, cg_ref, head_in, head_low, micro, row_len):
@@ -380,12 +397,13 @@
     same = (
         lax.broadcasted_iota(jnp.int32, (SW, SW), 0) // DH
         == lax.broadcasted_iota(jnp.int32, (SW, SW), 1) // DH
-    ).astype(F32)
+    )
+    same = jnp.where(same, 1.0, 0.0).astype(BF16)
     pooled, weights, members = [], [], []
     for m in range(micro):
         rows = slice(m * row_len, (m + 1) * row_len)
         s = head_in[rows, :]
-        e = exact(s * query, same) * scale
+        e = two_low(s * query, same) * scale
         sample = sample_column(ends_of(info, m), 0, row_len)
         share = jnp.zeros_like(e)
         for j in range(SAMP):
@@ -416,7 +434,7 @@
     sg_ref[D : D + SW, :] = exact(pooled, d_pre, (((0,), (0,)), ((), ())))
     sg_ref[D + SW + 1 : D + SW + 2, :] = row_sum(d_pre)
     d_pooled = exact(d_pre, pool_weight, (((1,), (1,)), ((), ())))
-    inner = exact(pooled * d_pooled, same)
+    inner = two_low(pooled * d_pooled, same)
     d_bias = jnp.zeros((1, SW), F32)
     d_query = jnp.zeros((1, SW), F32)
     for m in range(micro):
@@ -430,7 +448,7 @@
             spread = jnp.where(member, d_pooled[at : at + 1, :], spread)
             center = jnp.where(member, inner[at : at + 1, :], center)
         share = weights[m]
-        d_e = share * (exact(s * spread, same) - center) * scale
+        d_e = share * (two_low(s * spread, same) - center) * scale
         d_s = (share * spread + d_e * query).astype(BF16)
         head_low[rows, :] = d_s
         d_bias = d_bias + row_sum(d_s.astype(F32))
@@ -439,10 +457,10 @@
     sg_ref[D + SW + 2 : D + SW + 3, :] = d_query
 
 
-def feed(info, a1, blocks, vec, student, classifier, goals, send_row, send_col, returned):
-    micro, row_len, _ = a1.shape
+def feed(info, x, o, blocks, vec, student, classifier, goals, send_row, send_col, returned):
+    micro, row_len, _ = x.shape
     tokens = micro * row_len
-    tile = 256
+    tile = 512
     tiles = tokens // tile
     group, _, slots, _ = returned.shape
     whole = lambda *shape: pl.BlockSpec(shape, lambda i: (0,) * len(shape))
@@ -456,6 +474,7 @@
         grid=(2 * tiles,),
         in_specs=[
             pl.BlockSpec(memory_space=pltpu.SMEM),
+            ahead(D),
             ahead(D),
             once(NMAT, D, D),
             once(NMAT, D),
@@ -493,7 +512,6 @@
             pltpu.VMEM((tokens, D), BF16),
             pltpu.VMEM((tokens, SW), F32),
             pltpu.VMEM((tokens, SW), BF16),
-            pltpu.VMEM((tokens, D), BF16),
         ],
         compiler_params=pltpu.CompilerParams(vmem_limit_bytes=VMEM),
         cost_estimate=pl.CostEstimate(
@@ -501,7 +519,8 @@
         ),
     )(
         info,
-        a1.reshape(tokens, D),
+        x.reshape(tokens, D),
+        o.reshape(tokens, D),
         blocks,
         vec,
         student,
@@ -521,11 +540,13 @@
     k_ref,
     v_ref,
     o_ref,
+    l_ref,
     w_ref,
     _,
     dx_ref,
     wg_ref,
     vg_ref,
+    qx,
     kx,
     vx,
     dox,
@@ -540,6 +561,7 @@
     row_len = x_ref.shape[1]
     ends, live = ends_of(info, row), live_of(info, row)
     first = lane_index(QT) < DH
+    ones = jnp.ones((QT, LANES), F32)
 
     @pl.when(row == 0)
     def _():
@@ -558,63 +580,76 @@
     def _(t):
         rows = pl.ds(pl.multiple_of(t * QT, QT), QT)
         sample = sample_column(ends, t * QT, QT)
-        k_extra = key_spare(sample, QT)
+        lane = lane_index(QT) % DH
+        high, mid, rest = split_low(jnp.where(lane < PAIRS, -l_ref[0, rows, :], 0.0))
+        q_extra = (
+            query_spare(sample, QT)
+            + high
+            + pltpu.roll(mid, PAIRS, 1)
+            + pltpu.roll(rest, 2 * PAIRS, 1)
+        )
         branch = da1_ref[0, rows, :].astype(BF16)
         vg_ref[2:3, :] += row_sum(branch.astype(F32))
         do = nt(branch, w_ref[3]).astype(BF16).astype(F32)
         inner = do * o_ref[0, rows, :].astype(F32)
-        lane = lane_index(QT) % DH
         for p in range(PAIRS):
-            pair = slice(p * LANES, (p + 1) * LANES)
+            pair = head_lanes(p)
             high = inner[:, pair].astype(BF16)
             rest = (inner[:, pair] - high.astype(F32)).astype(BF16)
             delta = nn(high, crossed) + nn(rest, crossed)
-            high, mid, _rest = split_low(delta)
-            do_extra = jnp.where(lane == 0, -high, jnp.where(lane == 1, -mid, 0.0))
-            for ref, values, spare in (
-                (dox, do[:, pair], do_extra),
-                (kx, k_ref[0, rows, pair].astype(F32), k_extra),
-                (vx, v_ref[0, rows, pair].astype(F32), jnp.ones((QT, LANES), F32)),
-            ):
-                left, right = halves(values, spare, first)
-                ref[rows, 2 * p * LANES : (2 * p + 1) * LANES] = left.astype(BF16)
-                ref[rows, (2 * p + 1) * LANES : (2 * p + 2) * LANES] = right.astype(BF16)
+            high = delta.astype(BF16).astype(F32)
+            do_extra = jnp.where(lane == 0, -high, jnp.where(lane == 1, high - delta, 0.0))
+            store_heads(dox, rows, p, do[:, pair], do_extra, first)
+            store_heads(qx, rows, p, q_ref[0, rows, pair].astype(F32), q_extra, first)
+            store_heads(
+                kx, rows, p, k_ref[0, rows, pair].astype(F32), key_spare(sample, QT, p), first
+            )
+            store_heads(vx, rows, p, v_ref[0, rows, pair].astype(F32), ones, first)
 
     @pl.loop(0, row_len // QT)
     def _(t):
         rows = pl.ds(pl.multiple_of(t * QT, QT), QT)
-        begin, number = reach(ends, live, t * QT, QT, row_len)
+        begin, number = chosen_span(ends, live, t, row_len)
 
         @pl.when(number == 0)
         def _():
             dk[rows, :] = jnp.zeros((QT, D), BF16)
             dv[rows, :] = jnp.zeros((QT, D), BF16)
 
-        for n in range(1, row_len // KG + 1):
+        for n in widths(row_len):
 
             @pl.when(number == n)
             def _(n=n):
                 span = pl.ds(pl.multiple_of(begin * KG, KG), n * KG)
                 wide = lane_index(n * KG) < DH
-
-                @pl.loop(0, PAIRS)
-                def _(p):
-                    got = []
-                    for head in range(2):
-                        cols = pl.ds(
-                            pl.multiple_of((2 * p + head) * LANES, LANES), LANES
+                raw, done, got = {}, {}, {}
+                for step in range(H + 2):
+                    if step < H:
+                        cols = head_lanes(step)
+                        raw[step] = (
+                            nt(kx[rows, cols], qx[span, cols]),
+                            nt(vx[rows, cols], dox[span, cols]),
                         )
-                        q, k = q_ref[0, span, cols], kx[rows, cols]
-                        do = dox[span, cols]
-                        prob = jnp.exp(nt(k, q))
-                        ds = (prob * nt(vx[rows, cols], do)).astype(BF16)
-                        got.append(
-                            (nn(prob.astype(BF16), do), nn(ds, q), tn(ds, k))
+                    h = step - 1
+                    if 0 <= h < H:
+                        s, dp = raw.pop(h)
+                        prob = jnp.exp(s)
+                        done[h] = (prob.astype(BF16), (prob * dp).astype(BF16))
+                    h = step - 2
+                    if 0 <= h < H:
+                        cols = head_lanes(h)
+                        prob, ds = done.pop(h)
+                        got[h] = (
+                            nn(prob, dox[span, cols]),
+                            nn(ds, qx[span, cols]),
+                            tn(ds, kx[rows, cols]),
                         )
-                    cols = pl.ds(pl.multiple_of(p * LANES, LANES), LANES)
-                    dv[rows, cols] = jnp.where(first, got[0][0], got[1][0]).astype(BF16)
-                    dk[rows, cols] = jnp.where(first, got[0][1], got[1][1]).astype(BF16)
-                    dq[span, cols] += jnp.where(wide, got[0][2], got[1][2])
+                        if h % 2 == 1:
+                            left, right = got.pop(h - 1), got.pop(h)
+                            cols = head_lanes(h // 2)
+                            dv[rows, cols] = jnp.where(first, left[0], right[0]).astype(BF16)
+                            dk[rows, cols] = jnp.where(first, left[1], right[1]).astype(BF16)
+                            dq[span, cols] += jnp.where(wide, left[2], right[2])
 
     @pl.loop(0, row_len // QT)
     def _(t):
@@ -641,7 +676,7 @@
         wg_ref[...] = wsum[...].astype(BF16)
 
 
-def attend_back(info, tokens, da1, q, k, v, o, blocks, grads):
+def attend_back(info, tokens, da1, q, k, v, o, logs, blocks, grads):
     micro, row_len, _ = tokens.shape
     row_spec = lambda width: pl.BlockSpec((1, row_len, width), lambda r: (r, 0, 0))
     return pl.pallas_call(
@@ -649,12 +684,8 @@
         grid=(micro,),
         in_specs=[
             pl.BlockSpec(memory_space=pltpu.SMEM),
-            row_spec(D),
-            row_spec(D),
-            row_spec(2 * D),
-            row_spec(D),
-            row_spec(D),
-            row_spec(D),
+            *[row_spec(D)] * 6,
+            row_spec(LANES),
             pl.BlockSpec((4, D, D), lambda r: (0, 0, 0)),
             pl.BlockSpec(memory_space=pl.ANY),
         ],
@@ -669,22 +700,20 @@
             jax.ShapeDtypeStruct((8, D), F32),
         ],
         scratch_shapes=[
-            pltpu.VMEM((row_len, 2 * D), BF16),
-            pltpu.VMEM((row_len, 2 * D), BF16),
-            pltpu.VMEM((row_len, 2 * D), BF16),
+            *[pltpu.VMEM((row_len, 2 * D), BF16)] * 4,
             pltpu.VMEM((row_len, D), F32),
             pltpu.VMEM((row_len, D), BF16),
             pltpu.VMEM((row_len, D), BF16),
             pltpu.VMEM((4, D, D), F32),
         ],
-        input_output_aliases={8: 1},
+        input_output_aliases={9: 1},
         compiler_params=pltpu.CompilerParams(vmem_limit_bytes=VMEM),
         cost_estimate=pl.CostEstimate(
             flops=micro * row_len * D * D * 16 + micro * H * row_len * row_len * DH * 10,
             bytes_accessed=micro * row_len * D * 16,
             transcendentals=micro * H * row_len * row_len,
         ),
-    )(info, tokens, da1, q, k, v, o, blocks, grads)
+    )(info, tokens, da1, q, k, v, o, logs, blocks, grads)
 
 
 def pick_kernel(place_ref, rows_ref, out_ref):
@@ -1162,16 +1191,16 @@
     matrices = lax.all_gather(blocks, "shard", axis=0, tiled=True)
     vec = lax.all_gather(vectors.astype(BF16), "shard", axis=0, tiled=True).astype(F32)
 
-    a1, q, k, v, o = attend(info, tokens, matrices, vec)
+    q, k, v, o, logs = attend(info, tokens, matrices, vec)
     goals = jnp.concatenate(
         [teacher[:, 0], live[..., None].astype(F32)], axis=-1
     ).reshape(micro * SAMP, CLS + 1)
     da1, outgoing, ff_grads, ff_vecs, stu_grads, cls_grads = feed(
-        info, a1, matrices, vec, student, classifier, goals, send, send.reshape(-1, 1), returned
+        info, tokens, o, matrices, vec, student, classifier, goals, send, send.reshape(-1, 1), returned
     )
     arrived = lax.all_to_all(outgoing, "batch", split_axis=0, concat_axis=0, tiled=True)
     input_grads, grads, at_vecs = attend_back(
-        info, tokens, da1.reshape(micro, row_len, D), q, k, v, o, matrices, ff_grads
+        info, tokens, da1.reshape(micro, row_len, D), q, k, v, o, logs, matrices, ff_grads
     )
     layer_out = place_rows(back[:, None, :], arrived)
     own, vec_sum, stu_sum, cls_sum = reduce_grads(grads, ff_vecs, at_vecs, stu_grads, cls_grads)

time: 375 us -> 353 us (0.941); the launches traced: 375 us -> 348 us
  Pallas kernels: 300 us -> 268 us
  waiting for transfers between devices: 7.86 us -> 12.3 us
    pallas_call x1, Pallas kernels: 41.1 us -> 21.4 us  [attend(): pl.pallas_call(attend_kernel, grid=(micro,), in_specs=[pl.BlockSpec(memor...]
    pallas_call x1, Pallas kernels: 86.2 us -> 70.7 us  [feed(): pl.pallas_call(functools.partial(feed_kernel, tile=tile, micro=micro, row...]
    pallas_call x1, Pallas kernels: 52.8 us -> 62.5 us  [attend_back(): pl.pallas_call(functools.partial(attend_back_kernel, micro=micro), grid=(...]
    pallas_call x1, Pallas kernels: 95.8 us -> 89.3 us  [reduce_grads(): pl.pallas_call(functools.partial(reduce_kernel, group, owners), in_specs=...]
    all_to_all x1, waiting for transfers between devices: 0.01 us -> 4.04 us  [local(): lax.all_to_all(grad_outgoing, 'batch', split_axis=0, concat_axis=0, tiled...]
  transfers between devices with their start and end apart: 3 -> 3, of which waited for: 1 -> 2; matrix products, arithmetic and copies ran while one was open for 6% -> 6% of each run, Pallas kernels for 56% -> 55%
where the time goes in v3:
time: 353 us; the launch traced here: 348 us
  Pallas kernels  268 us (76%)
  blocking collectives  18.3 us (5%)
  between operations  15.2 us (4%)
  local copies, waits for them, and re-layouts  13.2 us (4%)
  waiting for transfers between devices  12.3 us (3%)
  starting transfers between devices  11.8 us (3%)
  other arithmetic  9.03 us (3%)
    pallas_call x1, Pallas kernels, reduce_grads(): pl.pallas_call(functools.partial(reduce_kernel, group, owners), in_specs=...  89.3 us
    pallas_call x1, Pallas kernels, feed(): pl.pallas_call(functools.partial(feed_kernel, tile=tile, micro=micro, row...  70.7 us
    pallas_call x1, Pallas kernels, attend_back(): pl.pallas_call(functools.partial(attend_back_kernel, micro=micro), grid=(...  62.5 us
    pallas_call x1, Pallas kernels, attend(): pl.pallas_call(attend_kernel, grid=(micro,), in_specs=[pl.BlockSpec(memor...  21.4 us
    pallas_call x1, Pallas kernels, update(): pl.pallas_call(functools.partial(update_kernel, owners=NMAT // per), grid...  14.8 us
    unnamed x1, blocking collectives  13.1 us
    unnamed x26, local copies, waits for them, and re-layouts  10.3 us
    all_gather x1, waiting for transfers between devices, local(): matrices = lax.all_gather(blocks, 'shard', axis=0, tiled=True)  7.56 us
  transfers between devices with their start and end apart: 3, of which 2 were waited for; matrix products, arithmetic and copies ran while one was open for 6% of the time, Pallas kernels for 55%

profile of v3, /device:TPU:0, one launch (start us, length us, event | category | flops | bytes accessed | tf_op | source)
XLA Modules:
  0.0 348.2 jit_solution(17521929067569083370)
XLA Ops:
  7.2 0.7 all-gather.4.cloned.1.call-update
  7.9 1.2 dynamic-slice
  9.8 0.7 broadcast_select_fusion
  10.5 0.8 fusion.25
  11.6 13.1 %all-reduce = s32[16]{0:T(128)S(1)} all-reduce(s32[16]{0:T(128)S(1)} %dynamic-update-slice), channel_id=2, replica_groups=mesh['batch'=8,'shard'=4] {'batch'}, use_global_device_ids=true, to_apply=%add | all-reduce | flops 16 | bytes 128
  25.0 0.9 reshape.505
  25.9 0.9 reshape.506
  26.8 2.1 fusion.8.place_ref
  28.9 5.0 %shard_map.272 = bf16[8,2,128,512]{3,2,1,0:T(8,128)(2,1)} custom-call(s32[2,1024,1]{2,1,0:T(8,128)} %fusion.8.place_ref, bf16[2,1024,512]{2,1,0:T(8,128)(2,1)} %bitcast.80), custom_call_target="tpu_custom_call" | custom-call | tf_op jit(solution)/shard_map/pallas_call | solution.py:730
  33.9 4.5 %all-to-all-start = ((bf16[8,2,128,512]{3,2,1,0:T(8,128)(2,1)}), bf16[8,2,128,512]{3,2,1,0:T(8,128)(2,1)}, u32[]{:S(2)}, u32[]{:S(2)}) async-start(bf16[8,2,128,512]{3,2,1,0:T(8,128)(2,1)} %shard_map.272), calls=%async_computation | async-start | bytes 4194304 | tf_op jit(solution)/shard_map/all_to_all | solution.py:1189
  38.6 5.2 %all-gather.1 = bf16[4,3,512]{2,1,0:T(4,128)(2,1)S(1)} all-gather(bf16[1,3,512]{2,1,0:T(4,128)(2,1)S(1)} %convert_bitcast_fusion), channel_id=1, replica_groups=mesh['batch'=8,'shard'=4] {'shard'}, dimensions={0}, use_global_device_ids=true | all-gather | bytes 15360 | tf_op jit(solution)/shard_map/all_gather | solution.py:1192
  43.8 0.6 reshape.502.vec_ref
  44.5 0.7 copy.111.cls_ref
  45.8 0.7 fusion.20
  47.8 0.6 pad_add_fusion.info
  48.4 0.7 pad_maximum_fusion.goal_ref
  49.1 2.1 fusion.3.send_col
  51.2 7.6 %all-gather.4.cloned.1.call-done.w_ref = bf16[12,512,512]{2,1,0:T(8,128)(2,1)} async-done(((bf16[3,512,512]{2,1,0:T(8,128)(2,1)}), bf16[12,512,512]{2,1,0:T(8,128)(2,1)}) %all-gather.4.cloned.1.call-update) | async-done | bytes 6291472 | tf_op jit(solution)/shard_map/all_gather | solution.py:1191
  58.8 21.4 %shard_map.271 = (bf16[2,1024,512]{2,1,0:T(8,128)(2,1)}, bf16[2,1024,512]{2,1,0:T(8,128)(2,1)}, bf16[2,1024,512]{2,1,0:T(8,128)(2,1)}, bf16[2,1024,512]{2,1,0:T(8,128)(2,1)}, f32[2,1024,128]{2,1,0:T(8,128)}) custom-call(s32[2,8]{1,0:T(2,128)} %pad_add_fusion.info, bf16[2,1024,512]{2,1,0:T(8,128)(2,1)} %bitcast.96, ...), custom_call_target="tpu_custom_call" | custom-call | flops 20401094656 | bytes 16777216 | tf_op jit(solution)/shard_map/pallas_call | solution.py:219
  80.2 4.0 %all-to-all-done.back_ref = bf16[8,2,128,512]{3,2,1,0:T(8,128)(2,1)} async-done(((bf16[8,2,128,512]{3,2,1,0:T(8,128)(2,1)}), bf16[8,2,128,512]{3,2,1,0:T(8,128)(2,1)}, u32[]{:S(2)}, u32[]{:S(2)}) %all-to-all-start) | async-done | bytes 2097184 | tf_op jit(solution)/shard_map/all_to_all | solution.py:1189
  84.2 70.7 %shard_map.273 = (f32[2048,512]{1,0:T(8,128)}, bf16[8,2,128,512]{3,2,1,0:T(8,128)(2,1)}, bf16[12,512,512]{2,1,0:T(8,128)(2,1)}, f32[12,512]{1,0:T(8,128)}, f32[643,128]{1,0:T(8,128)}, /*index=5*/f32[129,14]{1,0:T(8,128)}) custom-call(s32[2,8]{1,0:T(2,128)} %pad_add_fusion.info, bf16[2048,512]{1,0:T(8,128)(2,1)} %bitcast.97, bf16[2048,512]{1,0:T(8,128)(2,1)} %bitcast.101, ...), custom_call_target="tpu_custom_call" | custom-call | flops 25769803776 | bytes 16777216 | tf_op jit(solution)/shard_map/pallas_call | solution.py:472
  154.9 7.2 %all-to-all-start.1 = ((bf16[8,2,128,512]{3,2,1,0:T(8,128)(2,1)}), bf16[8,2,128,512]{3,2,1,0:T(8,128)(2,1)S(1)}, u32[]{:S(2)}, u32[]{:S(2)}) async-start(bf16[8,2,128,512]{3,2,1,0:T(8,128)(2,1)} %get-tuple-element.47), calls=%async_computation.1 | async-start | bytes 4194304 | tf_op jit(solution)/shard_map/all_to_all | solution.py:1201
  162.1 0.7 copy.113.cmom_ref
  162.8 0.7 compare_select_fusion.2.place_ref
  163.5 62.5 %shard_map.275 = (bf16[2,1024,512]{2,1,0:T(8,128)(2,1)}, bf16[12,512,512]{2,1,0:T(8,128)(2,1)}, f32[8,512]{1,0:T(8,128)}) custom-call(s32[2,8]{1,0:T(2,128)} %pad_add_fusion.info, bf16[2,1024,512]{2,1,0:T(8,128)(2,1)} %bitcast.98, f32[2,1024,512]{2,1,0:T(8,128)} %bitcast.99, ...), custom_call_target="tpu_custom_call", output_to_operand_aliasing={{1}: (9, {})} | custom-call | flops 19327352832 | bytes 16777216 | tf_op jit(solution)/shard_map/pallas_call | solution.py:682
  226.0 89.3 %shard_map.276 = (bf16[3,512,512]{2,1,0:T(8,128)(2,1)}, f32[16,512]{1,0:T(8,128)}, f32[656,128]{1,0:T(8,128)}, f32[144,128]{1,0:T(8,128)}) custom-call(bf16[12,512,512]{2,1,0:T(8,128)(2,1)} %get-tuple-element.55.grad_ref, f32[12,512]{1,0:T(8,128)} %get-tuple-element.56.ff_vec, f32[8,512]{1,0:T(8,128)} %get-tuple-element.57.at_vec, ...), custom_call_target="tpu_custom_call" | custom-call | flops 12582912 | bytes 25165824 | tf_op jit(solution)/shard_map/pallas_call | solution.py:1019
  315.3 14.8 %shard_map.277 = (f32[3,512,512]{2,1,0:T(8,128)}, f32[3,512,512]{2,1,0:T(8,128)}, f32[3,512,512]{2,1,0:T(8,128)}, f32[3,512,512]{2,1,0:T(8,128)}, f32[3,512]{1,0...) custom-call(bf16[3,512,512]{2,1,0:T(8,128)(2,1)} %get-tuple-element., ...), custom_call_target="tpu_custom_call" | custom-call | tf_op jit(solution)/shard_map/pallas_call | solution.py:1131
  330.2 1.6 copy.116
  331.7 1.6 copy.117
  333.3 1.6 copy.118
  334.9 1.4 copy-done
  336.2 4.7 %shard_map.274 = bf16[2,1024,512]{2,1,0:T(8,128)(2,1)} custom-call(s32[2,1,1024]{2,1,0:T(1,128)} %compare_select_fusion.2.place_ref, bf16[8,2,128,512]{3,2,1,0:T(8,128)(2,1)} %copy-done), custom_call_target="tpu_custom_call" | custom-call | tf_op jit(solution)/shard_map/pallas_call | solution.py:753
  (40 shorter events, 2.7 us)
Async XLA Ops:
  7.2 51.6 %all-gather.4.cloned.1.call-start = ((), (), s32[]{:S(2)}) async-start(), calls=%async_computation.2 | async-start | bytes 7864320 | tf_op jit(solution)/shard_map/all_gather | solution.py:1191
  33.9 4.5 %copy-start.2 = (s32[2,1,4]{2,1,0:T(1,128)S(1)}, s32[2,1,4]{2,1,0:T(1,128)}, u32[]{:S(2)}) copy-start(s32[2,1,4]{2,1,0:T(1,128)} %param.18) | copy-start | bytes 100
  33.9 4.7 %copy-start.1 = (f32[3,512]{1,0:T(4,128)S(1)}, f32[3,512]{1,0:T(4,128)}, u32[]{:S(2)}) copy-start(f32[3,512]{1,0:T(4,128)} %vec_ref.1) | copy-start | bytes 18436
  33.9 10.6 %copy-start.3 = (f32[129,14]{0,1:T(8,128)S(1)}, f32[129,14]{0,1:T(8,128)}, u32[]{:S(2)}) copy-start(f32[129,14]{0,1:T(8,128)} %param.30) | copy-start | bytes 21676
  33.9 50.3 %all-to-all-start = ((bf16[8,2,128,512]{3,2,1,0:T(8,128)(2,1)}), bf16[8,2,128,512]{3,2,1,0:T(8,128)(2,1)}, u32[]{:S(2)}, u32[]{:S(2)}) async-start(bf16[8,2,128,512]{3,2,1,0:T(8,128)(2,1)} %shard_map.272), calls=%async_computation | async-start | bytes 4194304 | tf_op jit(solution)/shard_map/all_to_all | solution.py:1189
  38.4 10.0 %copy-start.5 = (f32[2,1,4,14]{3,2,1,0:T(4,128)S(1)}, f32[2,1,4,14]{3,2,1,0:T(4,128)}, u32[]{:S(2)}) copy-start(f32[2,1,4,14]{3,2,1,0:T(4,128)} %param.20) | copy-start | bytes 1348
  154.9 7.2 %copy-start.4 = (f32[129,14]{0,1:T(8,128)S(1)}, f32[129,14]{0,1:T(8,128)}, u32[]{:S(2)}) copy-start(f32[129,14]{0,1:T(8,128)} %param.31) | copy-start | bytes 21676
  154.9 180.0 %all-to-all-start.1 = ((bf16[8,2,128,512]{3,2,1,0:T(8,128)(2,1)}), bf16[8,2,128,512]{3,2,1,0:T(8,128)(2,1)S(1)}, u32[]{:S(2)}, u32[]{:S(2)}) async-start(bf16[8,2,128,512]{3,2,1,0:T(8,128)(2,1)} %get-tuple-element.47), calls=%async_computation.1 | async-start | bytes 4194304 | tf_op jit(solution)/shard_map/all_to_all | solution.py:1201
  334.9 1.4 copy-start
Sparse Core Ops, SparseCore 0:
  9.6 49.1 all-gather.3
